TPU v7x, 512 devices: a whole 4x4x16 slice. The times are simulated.
512 devices in a mesh: node: 32 (over z, core), local: 16 (over x, y).
Axes of the slice: x: 4, y: 4, z: 16, core: 2. Of those that a mesh axis runs over, the one named last changes fastest.
Arguments:
- populations: float32 [512, 19, 4096], P(('node', 'local')), may hold values from 0.25 to 2.5, as said below
- fluid: int32 [512, 4096], P(('node', 'local')), may hold values 0 or 1
- neighbours: int32 [512, 6], P(('node', 'local')), may hold values from -1 to 511, as said below
Outputs:
- populations_out: float32 [512, 19, 4096], P(('node', 'local'))
- flow: float32 [3], replicated
Inputs may be any that keep to these rules, and one draw needn't show every extreme that they name: `populations`: every entry is positive. neighbours[b, k] is -1 or a block n other than b with neighbours[n, k ^ 1] = b; the owners b // 1 and n // 1 differ by at most 2, and by exactly 2 for some pairs.
All inputs are finite; a program needn't handle non-finite values. No bound on the sum of `fluid` on one device may be relied on, other than what follows from the above.
Results may differ from a plain program's by a relative error of at most 0.0003.
Values sent between devices are 32-bit elements; how exact they have to be, the bound alone decides.
No kernel may reach another device: no remote copies, remote signals or barrier semaphores. Data moves between devices by JAX's collectives and lax.ppermute only.
A program may use at most 64 MiB of HBM per device.

v0:
```python
import jax
import jax.numpy as jnp
import numpy as np
from jax import lax
from jax.sharding import PartitionSpec as P

BLK = 16
R = 2
SUBSTEPS = 2


VELOCITIES = (
    (0, 0, 0),
    (1, 0, 0),
    (-1, 0, 0),
    (0, 1, 0),
    (0, -1, 0),
    (0, 0, 1),
    (0, 0, -1),
    (1, 1, 0),
    (-1, -1, 0),
    (1, -1, 0),
    (-1, 1, 0),
    (1, 0, 1),
    (-1, 0, -1),
    (1, 0, -1),
    (-1, 0, 1),
    (0, 1, 1),
    (0, -1, -1),
    (0, 1, -1),
    (0, -1, 1),
)
WEIGHTS = (1.0 / 3.0,) + (1.0 / 18.0,) * 6 + (1.0 / 36.0,) * 12
OPPOSITE = (0, 2, 1, 4, 3, 6, 5, 8, 7, 10, 9, 12, 11, 14, 13, 16, 15, 18, 17)
OMEGA_PLUS = 1.6
MAGIC_PARAM = 0.1875


def from_behind(shard, axis, by):
    length = lax.axis_size(axis)
    pairs = [(i, i + by) for i in range(length) if 0 <= i + by < length]
    return lax.ppermute(shard, axis, pairs)


def outgoing(which_face):
    dim_num = which_face // 2
    sign_val = 1 if which_face % 2 else -1
    return [direction for direction in range(19) if VELOCITIES[direction][dim_num] == sign_val]


def collide(current, fluid):
    weights = jnp.array(WEIGHTS, dtype=jnp.float32)[:, None]
    lattice = jnp.array(VELOCITIES, dtype=jnp.float32)
    distribution = current * weights
    density = jnp.sum(distribution, axis=1)
    momentum = jnp.einsum("bic,id->bdc", distribution, lattice, precision=lax.Precision.HIGHEST)
    density_safe = jnp.where(fluid > 0, density, 1.0)
    velocity = momentum / density_safe[:, None, :]
    project = jnp.einsum("id,bdc->bic", lattice, velocity, precision=lax.Precision.HIGHEST)
    speed_sq = jnp.sum(velocity * velocity, axis=1)
    equilib = (
        weights
        * density[:, None, :]
        * (1.0 + 3.0 * project + 4.5 * project * project - 1.5 * speed_sq[:, None, :])
    )
    reverse = np.array(OPPOSITE)
    dist_rev = distribution[:, reverse]
    equil_rev = equilib[:, reverse]
    omega_minus = 1.0 / (MAGIC_PARAM / (1.0 / OMEGA_PLUS - 0.5) + 0.5)
    collided = (
        distribution
        - 0.5 * OMEGA_PLUS * (distribution + dist_rev - (equilib + equil_rev))
        - 0.5 * omega_minus * (distribution - dist_rev - (equilib - equil_rev))
    )
    return collided / weights


def face_tiles(collided, fluid, edge_len):
    blocks_here = collided.shape[0]
    cube = collided.reshape(blocks_here, 19, edge_len, edge_len, edge_len)
    wet_cube = fluid.reshape(blocks_here, edge_len, edge_len, edge_len).astype(jnp.float32)
    face_vals = []
    face_wet = []
    for face_num in range(6):
        dim_num = face_num // 2
        layer_at = edge_len - 1 if face_num % 2 else 0
        face_sheet = lax.index_in_dim(cube, layer_at, axis=2 + dim_num, keepdims=False)
        face_vals.append(
            face_sheet[:, np.array(outgoing(face_num))].reshape(blocks_here, 5, edge_len * edge_len)
        )
        wet_sheet = lax.index_in_dim(wet_cube, layer_at, axis=1 + dim_num, keepdims=False)
        face_wet.append(wet_sheet.reshape(blocks_here, edge_len * edge_len))
    return (jnp.stack(face_vals, axis=1), jnp.stack(face_wet, axis=1))


def wrap_cube(cube, sheets, edge_len):
    blocks_here = cube.shape[0]
    padded = cube
    for dim_num in range(3):
        sides = []
        for side_num in range(2):
            sheet = sheets[2 * dim_num + side_num]
            shape_now = list(padded.shape)
            shape_now[1 + dim_num] = 1
            if sheet is None:
                sides.append(jnp.zeros(tuple(shape_now), padded.dtype))
            else:
                grid = jnp.expand_dims(sheet.reshape(blocks_here, edge_len, edge_len), 1 + dim_num)
                widths = [(0, 0)] * 4
                for earlier in range(dim_num):
                    widths[1 + earlier] = (1, 1)
                sides.append(jnp.pad(grid, widths))
        padded = jnp.concatenate([sides[0], padded, sides[1]], axis=1 + dim_num)
    return padded


def source_view(padded, lattice_vec, edge_len):
    starts = [1 - lattice_vec[dim_num] for dim_num in range(3)]
    return padded[
        :,
        starts[0] : starts[0] + edge_len,
        starts[1] : starts[1] + edge_len,
        starts[2] : starts[2] + edge_len,
    ]


def stream_cells(collided, fluid, tiles_in, wet_in, edge_len):
    blocks_here = collided.shape[0]
    cell_count = edge_len**3
    wet_cell = fluid > 0
    wet_cube = fluid.reshape(blocks_here, edge_len, edge_len, edge_len).astype(jnp.float32)
    wet_pad = wrap_cube(wet_cube, [wet_in[:, face_num] for face_num in range(6)], edge_len)
    outputs = []
    for direction in range(19):
        lattice_vec = VELOCITIES[direction]
        if direction == 0:
            pulled = collided[:, 0]
        else:
            cube = collided[:, direction].reshape(blocks_here, edge_len, edge_len, edge_len)
            sheets = [None] * 6
            for dim_num in range(3):
                if lattice_vec[dim_num] != 0:
                    at_low = lattice_vec[dim_num] > 0
                    face_num = 2 * dim_num + (0 if at_low else 1)
                    slot_index = outgoing(face_num ^ 1).index(direction)
                    sheets[face_num] = tiles_in[:, face_num, slot_index]
            padded = wrap_cube(cube, sheets, edge_len)
            source_vals = source_view(padded, lattice_vec, edge_len).reshape(
                blocks_here, cell_count
            )
            source_wet = source_view(wet_pad, lattice_vec, edge_len).reshape(
                blocks_here, cell_count
            )
            pulled = jnp.where(source_wet > 0.5, source_vals, collided[:, OPPOSITE[direction]])
        outputs.append(jnp.where(wet_cell, pulled, 0.0))
    return jnp.stack(outputs, axis=1)


def shards(populations, fluid, neighbours):
    blocks_here = populations.shape[0]
    plane = BLK * BLK
    groups = lax.axis_size("local")
    curve_index = lax.axis_index("node") * groups + lax.axis_index("local")
    window_len = 2 * R + 1
    face_from = jnp.array([1, 0, 3, 2, 5, 4], dtype=jnp.int32)
    present = neighbours >= 0
    owner_slot = neighbours // blocks_here - curve_index + R
    flat_index = (owner_slot * blocks_here + neighbours % blocks_here) * 6 + face_from[None, :]
    flat_index = jnp.where(present, flat_index, 0)
    present_wet = present[:, :, None].astype(jnp.float32)
    current = populations
    for substep in range(SUBSTEPS):
        collided = collide(current, fluid)
        face_vals, face_wet = face_tiles(collided, fluid, BLK)
        moved_vals = []
        moved_wet = []
        for offset in range(-R, R + 1):
            if offset == 0:
                moved_vals.append(face_vals)
                moved_wet.append(face_wet)
            else:
                far_vals, far_wet = from_behind((face_vals, face_wet), ("node", "local"), -offset)
                moved_vals.append(far_vals)
                moved_wet.append(far_wet)
        window_vals = jnp.stack(moved_vals, axis=0)
        window_wet = jnp.stack(moved_wet, axis=0)
        window_vals = window_vals.reshape(window_len * blocks_here * 6, 5, plane)
        window_wet = window_wet.reshape(window_len * blocks_here * 6, plane)
        tiles_in = jnp.take(window_vals, flat_index, axis=0)
        wet_in = jnp.take(window_wet, flat_index, axis=0) * present_wet
        current = stream_cells(collided, fluid, tiles_in, wet_in, BLK)
    weights = jnp.array(WEIGHTS, dtype=jnp.float32)
    lattice = jnp.array(VELOCITIES, dtype=jnp.float32)
    direction_sums = jnp.sum(current, axis=(0, 2)) * weights
    local_momentum = jnp.dot(lattice.T, direction_sums, precision=lax.Precision.HIGHEST)
    total_momentum = lax.psum(local_momentum, ("node", "local"))
    block_total = blocks_here * lax.axis_size("node") * groups
    flow = total_momentum / (block_total * BLK * BLK)
    return (current, flow)


def solution(mesh):
    in_specs = (
        P(("node", "local"), None, None),
        P(("node", "local"), None),
        P(("node", "local"), None),
    )
    out_specs = (P(("node", "local"), None, None), P())
    return jax.shard_map(shards, mesh=mesh, in_specs=in_specs, out_specs=out_specs, check_vma=False)
```

profile of v0, /device:TPU:1, one launch (start us, length us, event | category | flops | bytes accessed | tf_op | source)
XLA Modules:
  0.0 301.2 jit_solution(10613231840846489926)
XLA Ops:
  9.2 3.1 %fusion.144 = (f32[1,19,16,16,1]{4,3,2,0,1:T(8,128)}, f32[1,19,16,16,1]{4,3,2,0,1:T(8,128)}) fusion(f32[1,19,16,16,16]{4,3,2,0,1:T(8,128)S(1)} %reshape.2004), kind=kLoop, calls=%fused_computation.563 | loop fusion | bytes 77824 | tf_op jit(solution)/shard_map/slice | solution.py:87
  17.5 3.5 %copy.171 = f32[1,19,16,16,1]{3,2,1,0,4:T(8,128)S(1)} copy(f32[1,19,16,16,1]{4,3,2,0,1:T(8,128)} %get-tuple-element.117) | data formatting | bytes 38912 | tf_op jit(solution)/shard_map/squeeze | solution.py:87
  22.4 1.8 copy.172
  27.8 5.6 %collective-permute-start.4 = (f32[1,6,5,256]{3,2,1,0:T(8,128)}, f32[1,6,5,256]{3,2,1,0:T(8,128)}, u32[]{:S(2)}, u32[]{:S(2)}) collective-permute-start(f32[1,6,5,256]{3,2,1,0:T(8,128)} %constant_dynamic-update-slice_fusion.5), channel_id=1, source_target_pairs={{0,2},{1,3},{2,4},{3,5},{4,6},{5,7},{6,8},{7,9},{8,10},{9,11},{10,... | collective-permute-start | bytes 92168 | tf_op jit(solution)/shard_map/ppermute | solution.py:42
  33.5 2.3 collective-permute-start.5
  35.8 6.6 %collective-permute-start.6 = (f32[1,6,5,256]{3,2,1,0:T(8,128)}, f32[1,6,5,256]{3,2,1,0:T(8,128)}, u32[]{:S(2)}, u32[]{:S(2)}) collective-permute-start(f32[1,6,5,256]{3,2,1,0:T(8,128)} %constant_dynamic-update-slice_fusion.5), channel_id=1, source_target_pairs={{1,0},{2,1},{3,2},{4,3},{5,4},{6,5},{7,6},{8,7},{9,8},{10,9},{11,1... | collective-permute-start | bytes 92168 | tf_op jit(solution)/shard_map/ppermute | solution.py:42
  42.4 2.4 collective-permute-start.7
  46.3 4.4 %collective-permute-start = (f32[1,6,256]{2,1,0:T(8,128)S(1)}, f32[1,6,256]{2,1,0:T(8,128)S(1)}, u32[]{:S(2)}, u32[]{:S(2)}) collective-permute-start(f32[1,6,256]{2,1,0:T(8,128)S(1)} %stack.193), channel_id=1, source_target_pairs={{0,2},{1,3},{2,4},{3,5},{4,6},{5,7},{6,8},{7,9},{8,10},{9,11},{10,... | collective-permute-start | bytes 18440 | tf_op jit(solution)/shard_map/ppermute | solution.py:42
  55.3 1.9 collective-permute-start.1
  57.3 6.4 %collective-permute-done.1 = f32[1,6,256]{2,1,0:T(8,128)S(1)} collective-permute-done((f32[1,6,256]{2,1,0:T(8,128)S(1)}, f32[1,6,256]{2,1,0:T(8,128)S(1)}, u32[]{:S(2)}, u32[]{:S(2)}) %collective-permute-start.1) | collective-permute-done | bytes 6176 | tf_op jit(solution)/shard_map/ppermute | solution.py:42
  63.6 1.9 collective-permute-start.2
  65.6 2.4 collective-permute-done.2
  68.0 3.4 %collective-permute-start.3 = (f32[1,6,256]{2,1,0:T(8,128)S(1)}, f32[1,6,256]{2,1,0:T(8,128)S(1)}, u32[]{:S(2)}, u32[]{:S(2)}) collective-permute-start(f32[1,6,256]{2,1,0:T(8,128)S(1)} %stack.193), channel_id=1, source_target_pairs={{2,0},{3,1},{4,2},{5,3},{6,4},{7,5},{8,6},{9,7},{10,8},{11,9},{12,... | collective-permute-start | bytes 18440 | tf_op jit(solution)/shard_map/ppermute | solution.py:42
  71.4 2.5 collective-permute-done.3
  95.0 1.6 fusion.69
  121.1 3.1 %fusion.142 = (f32[1,19,16,16,1]{4,3,2,0,1:T(8,128)}, f32[1,19,16,16,1]{4,3,2,0,1:T(8,128)}) fusion(f32[1,19,16,16,16]{4,3,2,0,1:T(8,128)S(1)} %reshape.2024), kind=kLoop, calls=%fused_computation.561 | loop fusion | bytes 77824 | tf_op jit(solution)/shard_map/slice | solution.py:87
  125.1 3.7 %copy.173 = f32[1,19,16,16,1]{3,2,1,0,4:T(8,128)S(1)} copy(f32[1,19,16,16,1]{4,3,2,0,1:T(8,128)} %get-tuple-element.111) | data formatting | bytes 38912 | tf_op jit(solution)/shard_map/squeeze | solution.py:87
  135.5 1.8 copy.174
  138.3 1.9 collective-permute-start.8
  140.3 3.2 %collective-permute-start.9 = (f32[1,6,5,256]{3,2,1,0:T(8,128)S(1)}, f32[1,6,5,256]{3,2,1,0:T(8,128)S(1)}, u32[]{:S(2)}, u32[]{:S(2)}) collective-permute-start(f32[1,6,5,256]{3,2,1,0:T(8,128)S(1)} %constant_dynamic-update-slice_fusion.19), channel_id=1, source_target_pairs={{0,1},{1,2},{2,3},{3,4},{4,5},{5,6},{6,7},{7,8},{8,9},{9,10},{10,1... | collective-permute-start | bytes 92168 | tf_op jit(solution)/shard_map/ppermute | solution.py:42
  143.5 7.2 %collective-permute-start.10 = (f32[1,6,5,256]{3,2,1,0:T(8,128)S(1)}, f32[1,6,5,256]{3,2,1,0:T(8,128)S(1)}, u32[]{:S(2)}, u32[]{:S(2)}) collective-permute-start(f32[1,6,5,256]{3,2,1,0:T(8,128)S(1)} %constant_dynamic-update-slice_fusion.19), channel_id=1, source_target_pairs={{1,0},{2,1},{3,2},{4,3},{5,4},{6,5},{7,6},{8,7},{9,8},{10,9},{11,1... | collective-permute-start | bytes 92168 | tf_op jit(solution)/shard_map/ppermute | solution.py:42
  150.7 4.8 %collective-permute-start.11 = (f32[1,6,5,256]{3,2,1,0:T(8,128)S(1)}, f32[1,6,5,256]{3,2,1,0:T(8,128)S(1)}, u32[]{:S(2)}, u32[]{:S(2)}) collective-permute-start(f32[1,6,5,256]{3,2,1,0:T(8,128)S(1)} %constant_dynamic-update-slice_fusion.19), channel_id=1, source_target_pairs={{2,0},{3,1},{4,2},{5,3},{6,4},{7,5},{8,6},{9,7},{10,8},{11,9},{12,... | collective-permute-start | bytes 92168 | tf_op jit(solution)/shard_map/ppermute | solution.py:42
  159.5 1.6 gather_fusion.18
  182.3 118.3 %psum.7 = f32[3]{0:T(128)S(1)} all-reduce(f32[3]{0:T(128)S(1)} %convolution_bitcast_fusion.2), channel_id=1, replica_groups=mesh['node'=32,'local'=16] {'node','local'}, use_global_device_ids=true, to_apply=%region_5.8 | all-reduce | flops 3 | bytes 24 | tf_op jit(solution)/shard_map/psum | solution.py:196
  (484 shorter events, 102.3 us)
Async XLA Ops:
  21.1 30.4 %copy-start.79 = (s32[1,6]{1,0:T(1,128)S(1)}, s32[1,6]{1,0:T(1,128)}, u32[]{:S(2)}) copy-start(s32[1,6]{1,0:T(1,128)} %param.46) | copy-start | bytes 76
  21.1 30.4 %copy-start.80 = (s32[1,6]{1,0:T(1,128)S(1)}, s32[1,6]{1,0:T(1,128)}, u32[]{:S(2)}) copy-start(s32[1,6]{1,0:T(1,128)} %constant.216) | copy-start | bytes 76
  21.1 32.9 %copy-start.61 = (s32[1024]{0:T(1024)}, s32[1024]{0:T(1024)S(1)}, u32[]{:S(2)}) copy-start(s32[1024]{0:T(1024)S(1)} %get-tuple-element.210) | copy-start | bytes 12292
  27.8 59.0 %collective-permute-start.4 = (f32[1,6,5,256]{3,2,1,0:T(8,128)}, f32[1,6,5,256]{3,2,1,0:T(8,128)}, u32[]{:S(2)}, u32[]{:S(2)}) collective-permute-start(f32[1,6,5,256]{3,2,1,0:T(8,128)} %constant_dynamic-update-slice_fusion.5), channel_id=1, source_target_pairs={{0,2},{1,3},{2,4},{3,5},{4,6},{5,7},{6,8},{7,9},{8,10},{9,11},{10,... | collective-permute-start | bytes 92168 | tf_op jit(solution)/shard_map/ppermute | solution.py:42
  33.5 54.2 %collective-permute-start.5 = (f32[1,6,5,256]{3,2,1,0:T(8,128)}, f32[1,6,5,256]{3,2,1,0:T(8,128)}, u32[]{:S(2)}, u32[]{:S(2)}) collective-permute-start(f32[1,6,5,256]{3,2,1,0:T(8,128)} %constant_dynamic-update-slice_fusion.5), channel_id=1, source_target_pairs={{0,1},{1,2},{2,3},{3,4},{4,5},{5,6},{6,7},{7,8},{8,9},{9,10},{10,1... | collective-permute-start | bytes 92168 | tf_op jit(solution)/shard_map/ppermute | solution.py:42
  35.8 53.5 %collective-permute-start.6 = (f32[1,6,5,256]{3,2,1,0:T(8,128)}, f32[1,6,5,256]{3,2,1,0:T(8,128)}, u32[]{:S(2)}, u32[]{:S(2)}) collective-permute-start(f32[1,6,5,256]{3,2,1,0:T(8,128)} %constant_dynamic-update-slice_fusion.5), channel_id=1, source_target_pairs={{1,0},{2,1},{3,2},{4,3},{5,4},{6,5},{7,6},{8,7},{9,8},{10,9},{11,1... | collective-permute-start | bytes 92168 | tf_op jit(solution)/shard_map/ppermute | solution.py:42
  42.4 47.7 %collective-permute-start.7 = (f32[1,6,5,256]{3,2,1,0:T(8,128)}, f32[1,6,5,256]{3,2,1,0:T(8,128)}, u32[]{:S(2)}, u32[]{:S(2)}) collective-permute-start(f32[1,6,5,256]{3,2,1,0:T(8,128)} %constant_dynamic-update-slice_fusion.5), channel_id=1, source_target_pairs={{2,0},{3,1},{4,2},{5,3},{6,4},{7,5},{8,6},{9,7},{10,8},{11,9},{12,... | collective-permute-start | bytes 92168 | tf_op jit(solution)/shard_map/ppermute | solution.py:42
  46.3 9.1 %collective-permute-start = (f32[1,6,256]{2,1,0:T(8,128)S(1)}, f32[1,6,256]{2,1,0:T(8,128)S(1)}, u32[]{:S(2)}, u32[]{:S(2)}) collective-permute-start(f32[1,6,256]{2,1,0:T(8,128)S(1)} %stack.193), channel_id=1, source_target_pairs={{0,2},{1,3},{2,4},{3,5},{4,6},{5,7},{6,8},{7,9},{8,10},{9,11},{10,... | collective-permute-start | bytes 18440 | tf_op jit(solution)/shard_map/ppermute | solution.py:42
  51.6 39.9 %copy-start.54 = (pred[6]{0:T(512)(128)(4,1)}, pred[6]{0:T(512)(128)(4,1)S(1)}, u32[]{:S(2)}) copy-start(pred[6]{0:T(512)(128)(4,1)S(1)} %get-tuple-element.108) | copy-start | bytes 22
  51.6 39.3 %copy-start.56 = (s32[1024]{0:T(1024)}, s32[1024]{0:T(1024)S(1)}, u32[]{:S(2)}) copy-start(s32[1024]{0:T(1024)S(1)} %pad_clamp_fusion.6) | copy-start | bytes 12292
  55.3 8.3 %collective-permute-start.1 = (f32[1,6,256]{2,1,0:T(8,128)S(1)}, f32[1,6,256]{2,1,0:T(8,128)S(1)}, u32[]{:S(2)}, u32[]{:S(2)}) collective-permute-start(f32[1,6,256]{2,1,0:T(8,128)S(1)} %stack.193), channel_id=1, source_target_pairs={{0,1},{1,2},{2,3},{3,4},{4,5},{5,6},{6,7},{7,8},{8,9},{9,10},{10,1... | collective-permute-start | bytes 18440 | tf_op jit(solution)/shard_map/ppermute | solution.py:42
  63.6 4.4 %collective-permute-start.2 = (f32[1,6,256]{2,1,0:T(8,128)S(1)}, f32[1,6,256]{2,1,0:T(8,128)S(1)}, u32[]{:S(2)}, u32[]{:S(2)}) collective-permute-start(f32[1,6,256]{2,1,0:T(8,128)S(1)} %stack.193), channel_id=1, source_target_pairs={{1,0},{2,1},{3,2},{4,3},{5,4},{6,5},{7,6},{8,7},{9,8},{10,9},{11,1... | collective-permute-start | bytes 18440 | tf_op jit(solution)/shard_map/ppermute | solution.py:42
  68.0 5.9 %collective-permute-start.3 = (f32[1,6,256]{2,1,0:T(8,128)S(1)}, f32[1,6,256]{2,1,0:T(8,128)S(1)}, u32[]{:S(2)}, u32[]{:S(2)}) collective-permute-start(f32[1,6,256]{2,1,0:T(8,128)S(1)} %stack.193), channel_id=1, source_target_pairs={{2,0},{3,1},{4,2},{5,3},{6,4},{7,5},{8,6},{9,7},{10,8},{11,9},{12,... | collective-permute-start | bytes 18440 | tf_op jit(solution)/shard_map/ppermute | solution.py:42
  77.5 37.8 %copy-start.15 = (pred[1,4096]{1,0:T(4,128)(4,1)}, pred[1,4096]{1,0:T(4,128)(4,1)S(1)}, u32[]{:S(2)}) copy-start(pred[1,4096]{1,0:T(4,128)(4,1)S(1)} %gt.374) | copy-start | bytes 12292
  77.6 37.6 %copy-start.13 = (pred[1,4096]{1,0:T(4,128)(4,1)}, pred[1,4096]{1,0:T(4,128)(4,1)S(1)}, u32[]{:S(2)}) copy-start(pred[1,4096]{1,0:T(4,128)(4,1)S(1)} %gt.378) | copy-start | bytes 12292
  77.8 37.5 %copy-start.11 = (pred[1,4096]{1,0:T(4,128)(4,1)}, pred[1,4096]{1,0:T(4,128)(4,1)S(1)}, u32[]{:S(2)}) copy-start(pred[1,4096]{1,0:T(4,128)(4,1)S(1)} %gt.382) | copy-start | bytes 12292
  77.9 37.4 %copy-start.9 = (pred[1,4096]{1,0:T(4,128)(4,1)}, pred[1,4096]{1,0:T(4,128)(4,1)S(1)}, u32[]{:S(2)}) copy-start(pred[1,4096]{1,0:T(4,128)(4,1)S(1)} %gt.384) | copy-start | bytes 12292
  80.2 35.4 %copy-start.19 = (pred[1,4096]{1,0:T(4,128)(4,1)}, pred[1,4096]{1,0:T(4,128)(4,1)S(1)}, u32[]{:S(2)}) copy-start(pred[1,4096]{1,0:T(4,128)(4,1)S(1)} %gt.376) | copy-start | bytes 12292
  80.3 35.2 %copy-start.17 = (pred[1,4096]{1,0:T(4,128)(4,1)}, pred[1,4096]{1,0:T(4,128)(4,1)S(1)}, u32[]{:S(2)}) copy-start(pred[1,4096]{1,0:T(4,128)(4,1)S(1)} %gt.380) | copy-start | bytes 12292
  138.3 20.4 %collective-permute-start.8 = (f32[1,6,5,256]{3,2,1,0:T(8,128)S(1)}, f32[1,6,5,256]{3,2,1,0:T(8,128)S(1)}, u32[]{:S(2)}, u32[]{:S(2)}) collective-permute-start(f32[1,6,5,256]{3,2,1,0:T(8,128)S(1)} %constant_dynamic-update-slice_fusion.19), channel_id=1, source_target_pairs={{0,2},{1,3},{2,4},{3,5},{4,6},{5,7},{6,8},{7,9},{8,10},{9,11},{10,... | collective-permute-start | bytes 92168 | tf_op jit(solution)/shard_map/ppermute | solution.py:42
  140.3 18.5 %collective-permute-start.9 = (f32[1,6,5,256]{3,2,1,0:T(8,128)S(1)}, f32[1,6,5,256]{3,2,1,0:T(8,128)S(1)}, u32[]{:S(2)}, u32[]{:S(2)}) collective-permute-start(f32[1,6,5,256]{3,2,1,0:T(8,128)S(1)} %constant_dynamic-update-slice_fusion.19), channel_id=1, source_target_pairs={{0,1},{1,2},{2,3},{3,4},{4,5},{5,6},{6,7},{7,8},{8,9},{9,10},{10,1... | collective-permute-start | bytes 92168 | tf_op jit(solution)/shard_map/ppermute | solution.py:42
  143.5 15.3 %collective-permute-start.10 = (f32[1,6,5,256]{3,2,1,0:T(8,128)S(1)}, f32[1,6,5,256]{3,2,1,0:T(8,128)S(1)}, u32[]{:S(2)}, u32[]{:S(2)}) collective-permute-start(f32[1,6,5,256]{3,2,1,0:T(8,128)S(1)} %constant_dynamic-update-slice_fusion.19), channel_id=1, source_target_pairs={{1,0},{2,1},{3,2},{4,3},{5,4},{6,5},{7,6},{8,7},{9,8},{10,9},{11,1... | collective-permute-start | bytes 92168 | tf_op jit(solution)/shard_map/ppermute | solution.py:42
  150.7 8.1 %collective-permute-start.11 = (f32[1,6,5,256]{3,2,1,0:T(8,128)S(1)}, f32[1,6,5,256]{3,2,1,0:T(8,128)S(1)}, u32[]{:S(2)}, u32[]{:S(2)}) collective-permute-start(f32[1,6,5,256]{3,2,1,0:T(8,128)S(1)} %constant_dynamic-update-slice_fusion.19), channel_id=1, source_target_pairs={{2,0},{3,1},{4,2},{5,3},{6,4},{7,5},{8,6},{9,7},{10,8},{11,9},{12,... | collective-permute-start | bytes 92168 | tf_op jit(solution)/shard_map/ppermute | solution.py:42
  181.9 119.2 %copy-start.8 = (f32[1,19,4096]{2,0,1:T(1,128)}, f32[1,19,4096]{2,0,1:T(1,128)S(1)}, u32[]{:S(2)}) copy-start(f32[1,19,4096]{2,0,1:T(1,128)S(1)} %constant_dynamic-update-slice_fusion.30) | copy-start | bytes 933892
  (70 other events, 503.0 us)
where the time goes:
time: 303 us; the launch traced here: 301 us
  blocking collectives  118 us (39%)
  local copies, waits for them, and re-layouts  105 us (35%)
  starting transfers between devices  45.7 us (15%)
  other arithmetic  13.6 us (4%)
  waiting for transfers between devices  11.3 us (4%)
  matrix products  3.92 us (1%)
  between operations  3.29 us (1%)
    psum x1, blocking collectives, shards(): total_momentum = lax.psum(local_momentum, ('node', 'local'))  118 us
    ppermute x12, starting transfers between devices, from_behind(): return lax.ppermute(shard, axis, pairs)  45.7 us
    another operation x66, local copies, waits for them, and re-layouts, wrap_cube(): jnp.expand_dims(sheet.reshape(blocks_here, edge_len, edge_len), 1 + dim_num)  27.8 us
    squeeze x6, local copies, waits for them, and re-layouts, face_tiles(): lax.index_in_dim(cube, layer_at, axis=2 + dim_num, keepdims=False)  11.6 us
    ppermute x12, waiting for transfers between devices, from_behind(): return lax.ppermute(shard, axis, pairs)  11.3 us
    gt x18, local copies, waits for them, and re-layouts, stream_cells(): source_wet > 0.5  10.1 us
    gather x12, local copies, waits for them, and re-layouts, face_tiles(): face_sheet[:, np.array(outgoing(face_num))]  9.65 us
    unnamed x188, local copies, waits for them, and re-layouts  9.3 us
  transfers between devices with their start and end apart: 12, of which 3 were waited for; matrix products, arithmetic and copies ran while one was open for 8% of the time, Pallas kernels for 0%

commit v1 on v0

v1 whole, which is shorter than its diff:
```python
import functools

import jax
import jax.numpy as jnp
from jax import lax
from jax.experimental import pallas as pl
from jax.experimental.pallas import tpu as pltpu
from jax.sharding import PartitionSpec as P

BLK = 16
R = 2

VELOCITIES = (
    (0, 0, 0),
    (1, 0, 0),
    (-1, 0, 0),
    (0, 1, 0),
    (0, -1, 0),
    (0, 0, 1),
    (0, 0, -1),
    (1, 1, 0),
    (-1, -1, 0),
    (1, -1, 0),
    (-1, 1, 0),
    (1, 0, 1),
    (-1, 0, -1),
    (1, 0, -1),
    (-1, 0, 1),
    (0, 1, 1),
    (0, -1, -1),
    (0, 1, -1),
    (0, -1, 1),
)
WEIGHTS = (1.0 / 3.0,) + (1.0 / 18.0,) * 6 + (1.0 / 36.0,) * 12
OPPOSITE = (0, 2, 1, 4, 3, 6, 5, 8, 7, 10, 9, 12, 11, 14, 13, 16, 15, 18, 17)
OMEGA_PLUS = 1.6
MAGIC_PARAM = 0.1875
OMEGA_MINUS = 1.0 / (MAGIC_PARAM / (1.0 / OMEGA_PLUS - 0.5) + 0.5)
STRIDES = (256, 16, 1)

ROWS, LANES = 32, 128
PACK_ROWS = 88
Y_AT, Z_AT, X_LOW_AT, X_HIGH_AT = 0, 32, 64, 76
WET_SLOT = 5
BIG = 3.0e38
LIMIT = 1.0e38


def outgoing(face):
    sign = 1 if face % 2 else -1
    return [i for i in range(19) if VELOCITIES[i][face // 2] == sign]


class Grid:
    def __init__(self):
        self.row = lax.broadcasted_iota(jnp.int32, (ROWS, LANES), 0)
        self.lane = lax.broadcasted_iota(jnp.int32, (ROWS, LANES), 1)
        self.flat = self.row * LANES + self.lane
        self.odd = (self.row & 1) == 1
        self.z = self.lane & 15
        self.slot = self.lane >> 4

    def plane(self, dim, sign):
        if dim == 1:
            return self.odd & (self.slot == 7) if sign > 0 else (~self.odd) & (self.slot == 0)
        return self.z == (15 if sign > 0 else 0)

    def beyond(self, dim, sign, other, other_sign):
        source = (self.flat + sign * STRIDES[dim]) & 4095
        coord = source >> 8 if other == 0 else (source >> 4) & 15
        return coord != (15 if other_sign > 0 else 0)


def lane_roll(a, t):
    t %= LANES
    return a if t == 0 else pltpu.roll(a, t, 1)


def row_roll(a, q):
    q %= ROWS
    return a if q == 0 else pltpu.roll(a, q, 0)


def flat_roll(grid, a, shift):
    q, t = divmod(shift % 4096, LANES)
    if t == 0:
        return row_roll(a, q)
    rolled = lane_roll(a, t)
    return jnp.where(grid.lane >= t, row_roll(rolled, q), row_roll(rolled, q + 1))


def collide(g, wet):
    rho = g[0] * WEIGHTS[0]
    rho = rho + (g[1] + g[2] + g[3] + g[4] + g[5] + g[6]) * WEIGHTS[1]
    diagonal = g[7]
    for i in range(8, 19):
        diagonal = diagonal + g[i]
    rho = rho + diagonal * WEIGHTS[7]
    inverse = 1.0 / jnp.where(wet, rho, 1.0)
    u = []
    for dim in range(3):
        axis_part = diag_part = None
        for i in range(1, 19, 2):
            c = VELOCITIES[i][dim]
            if c == 0:
                continue
            diff = g[i] - g[i + 1] if c > 0 else g[i + 1] - g[i]
            if i < 7:
                axis_part = diff
            else:
                diag_part = diff if diag_part is None else diag_part + diff
        u.append((axis_part * WEIGHTS[1] + diag_part * WEIGHTS[7]) * inverse)
    speed_sq = u[0] * u[0] + u[1] * u[1] + u[2] * u[2]
    base = 1.0 - 1.5 * speed_sq
    out = [None] * 19
    out[0] = g[0] - (0.5 * OMEGA_PLUS) * (2.0 * g[0] - 2.0 * rho * base)
    for i in range(1, 19, 2):
        project = None
        for dim in range(3):
            c = VELOCITIES[i][dim]
            if c > 0:
                project = u[dim] if project is None else project + u[dim]
            elif c < 0:
                project = project - u[dim]
        even = (0.5 * OMEGA_PLUS) * ((g[i] + g[i + 1]) - 2.0 * rho * (base + 4.5 * project * project))
        odd = (0.5 * OMEGA_MINUS) * ((g[i] - g[i + 1]) - 6.0 * rho * project)
        out[i] = g[i] - even - odd
        out[i + 1] = g[i + 1] - even + odd
    return out


def write_pack(grid, g, wet, pack_ref):
    wet_value = jnp.where(wet, 1.0, 0.0)

    def of(face):
        return [g[i] for i in outgoing(face)] + [wet_value]

    low, high = of(2), of(3)
    pack = jnp.zeros((ROWS, LANES), jnp.float32)
    for j in range(6):
        both = jnp.where(grid.odd, lane_roll(high[j], 16 * (j + 1)), lane_roll(low[j], 16 * j))
        pack = jnp.where(grid.slot == j, both, pack)
    pack_ref[Y_AT : Y_AT + ROWS, :] = jnp.where(grid.odd, row_roll(pack, -2), row_roll(pack, 2))
    low, high = of(4), of(5)
    pack = jnp.zeros((ROWS, LANES), jnp.float32)
    for j in range(6):
        pack = jnp.where(grid.z == j, lane_roll(low[j], j), pack)
        pack = jnp.where(grid.z == 8 + j, lane_roll(high[j], j - 7), pack)
    pack_ref[Z_AT : Z_AT + ROWS, :] = jnp.where(
        grid.z >= 8, flat_roll(grid, pack, -16), flat_roll(grid, pack, 16)
    )
    low, high = of(0), of(1)
    for j in range(6):
        pack_ref[X_LOW_AT + 2 * j : X_LOW_AT + 2 * j + 2, :] = low[j][0:2, :]
        pack_ref[X_HIGH_AT + 2 * j : X_HIGH_AT + 2 * j + 2, :] = high[j][30:32, :]


def pair_mate(me):
    return me ^ 1


def other_side(me):
    return ((me + 1) ^ 1) - 1


def pull(grid, wet, own_ref, nb_ref, pack_refs, work_ref, put):
    me = lax.axis_index("node") * lax.axis_size("local") + lax.axis_index("local")
    sources = [other_side(me), pair_mate(me), other_side(pair_mate(me)), pair_mate(other_side(me))]

    def select(face, start, rows):
        block = nb_ref[0, face]
        value = jnp.zeros((rows, LANES), jnp.float32)
        for source, ref in zip(sources, pack_refs):
            value = jnp.where((block >= 0) & (block == source), ref[start : start + rows, :], value)
        return value

    ghost_y = jnp.where(grid.odd, select(2, Y_AT, ROWS), select(3, Y_AT, ROWS))
    ghost_z = jnp.where(grid.z >= 8, select(4, Z_AT, ROWS), select(5, Z_AT, ROWS))
    ghost_x = {1: select(0, X_HIGH_AT, 12), -1: select(1, X_LOW_AT, 12)}
    wet_y = {
        1: lane_roll(ghost_y, 112 - 16 * WET_SLOT) > 0.5,
        -1: lane_roll(ghost_y, -16 * WET_SLOT) > 0.5,
    }
    wet_z = {
        1: lane_roll(ghost_z, 7 - WET_SLOT) > 0.5,
        -1: lane_roll(ghost_z, -WET_SLOT) > 0.5,
    }
    wet_x = {s: ghost_x[s][2 * WET_SLOT : 2 * WET_SLOT + 2, :] > 0.5 for s in (1, -1)}
    put(0, jnp.where(wet, own_ref[0], 0.0), None)
    for i in range(1, 19):
        c = VELOCITIES[i]
        a = own_ref[i]
        if c[0] != 0:
            j = outgoing(1 if c[0] > 0 else 0).index(i)
            at = 30 if c[0] > 0 else 0
            work_ref[i] = a
            work_ref[i, at : at + 2, :] = jnp.where(
                wet_x[c[0]], ghost_x[c[0]][2 * j : 2 * j + 2, :], BIG
            )
            a = work_ref[i]
        if c[1] != 0:
            j = outgoing(3 if c[1] > 0 else 2).index(i)
            ghost = lane_roll(ghost_y, 112 - 16 * j if c[1] > 0 else -16 * j)
            fine = wet_y[c[1]]
            if c[0] != 0:
                fine = fine & grid.beyond(1, c[1], 0, c[0])
            a = jnp.where(grid.plane(1, c[1]), jnp.where(fine, ghost, BIG), a)
        if c[2] != 0:
            j = outgoing(5 if c[2] > 0 else 4).index(i)
            ghost = lane_roll(ghost_z, 7 - j if c[2] > 0 else -j)
            fine = wet_z[c[2]]
            for other in (0, 1):
                if c[other] != 0:
                    fine = fine & grid.beyond(2, c[2], other, c[other])
            a = jnp.where(grid.plane(2, c[2]), jnp.where(fine, ghost, BIG), a)
        moved = flat_roll(grid, a, sum(c[d] * STRIDES[d] for d in range(3)))
        open_link = moved < LIMIT
        value = jnp.where(open_link, moved, own_ref[OPPOSITE[i]])
        put(i, jnp.where(wet, value, 0.0), open_link)


def first_kernel(pop_hbm, fluid_hbm, post_ref, pack_ref, pop_ref, fluid_ref, sems):
    pop_copy = pltpu.make_async_copy(pop_hbm, pop_ref, sems.at[0])
    fluid_copy = pltpu.make_async_copy(fluid_hbm, fluid_ref, sems.at[1])
    pop_copy.start()
    fluid_copy.start()
    fluid_copy.wait()
    pop_copy.wait()
    grid = Grid()
    wet = fluid_ref[...] > 0
    g = collide([pop_ref[i] for i in range(19)], wet)
    for i in range(19):
        post_ref[i] = jnp.where(wet, g[i], BIG)
    write_pack(grid, g, wet, pack_ref)


def pack_kernel(post_ref, fluid_ref, pack_ref):
    wet = fluid_ref[...] > 0
    write_pack(Grid(), [jnp.where(wet, post_ref[i], 0.0) for i in range(19)], wet, pack_ref)


def middle_kernel(own_ref, fluid_ref, nb_ref, p0, p1, p2, p3, post_ref, sum_ref, work_ref, now_ref, sign_ref):
    grid = Grid()
    wet = fluid_ref[...] > 0

    def put(i, value, open_link):
        now_ref[i] = value
        if i:
            sign_ref[i] = jnp.where(wet, jnp.where(open_link, 1.0, -1.0), 0.0)

    pull(grid, wet, own_ref, nb_ref, (p0, p1, p2, p3), work_ref, put)
    g = collide([now_ref[i] for i in range(19)], wet)
    for i in range(19):
        post_ref[i] = jnp.where(wet, g[i], BIG)
    totals = [None] * 3
    for i in range(1, 19, 2):
        signed = (g[i] * sign_ref[i + 1] - g[i + 1] * sign_ref[i]) * WEIGHTS[i]
        for dim in range(3):
            c = VELOCITIES[i][dim]
            if c > 0:
                totals[dim] = signed if totals[dim] is None else totals[dim] + signed
            elif c < 0:
                totals[dim] = -signed if totals[dim] is None else totals[dim] - signed
    lane = lax.broadcasted_iota(jnp.int32, sum_ref.shape, 2)
    line = jnp.zeros(sum_ref.shape, jnp.float32)
    for dim in range(3):
        total = jnp.sum(jnp.sum(totals[dim], axis=0, keepdims=True), axis=1, keepdims=True)[None]
        line = jnp.where(lane == dim, total, line)
    sum_ref[...] = line


def last_kernel(own_ref, fluid_ref, nb_ref, p0, p1, p2, p3, out_ref, work_ref):
    grid = Grid()
    wet = fluid_ref[...] > 0

    def put(i, value, open_link):
        out_ref[i] = value

    pull(grid, wet, own_ref, nb_ref, (p0, p1, p2, p3), work_ref, put)


def vmem(count):
    return [pl.BlockSpec(memory_space=pltpu.VMEM)] * count


def swap(pack, partner):
    length = lax.axis_size("node") * lax.axis_size("local")
    pairs = [(i, partner(i)) for i in range(length) if 0 <= partner(i) < length]
    return lax.ppermute(pack, ("node", "local"), pairs)


def exchange(pack):
    other = swap(pack, other_side)
    mate = swap(pack, pair_mate)
    return [other, mate]


def pass_on(other, mate):
    past_mate = swap(other, pair_mate)
    past_other = swap(mate, other_side)
    return [other, mate, past_mate, past_other]


def spread_out(lines, axis):
    return lax.all_to_all(lines, axis, 0, 0, tiled=True)


def shards(populations, fluid, neighbours):
    f32 = jnp.float32
    cube = jax.ShapeDtypeStruct((19, ROWS, LANES), f32)
    packed = jax.ShapeDtypeStruct((PACK_ROWS, LANES), f32)
    lines = jax.ShapeDtypeStruct((lax.axis_size("local"), 8, LANES), f32)
    scratch = pltpu.VMEM((19, ROWS, LANES), f32)
    smem = [pl.BlockSpec(memory_space=pltpu.SMEM)]
    devices = lax.axis_size("node") * lax.axis_size("local")
    params = pltpu.CompilerParams(vmem_limit_bytes=16 * 2**20)
    pop = populations.reshape(19, ROWS, LANES)
    wall = fluid.reshape(ROWS, LANES)

    post, pack = pl.pallas_call(
        first_kernel,
        out_shape=(cube, packed),
        in_specs=[pl.BlockSpec(memory_space=pltpu.HBM)] * 2,
        out_specs=tuple(vmem(2)),
        scratch_shapes=[scratch, pltpu.VMEM((ROWS, LANES), jnp.int32), pltpu.SemaphoreType.DMA((2,))],
        compiler_params=params,
        name="collide_first",
    )(pop, wall)
    ghosts = pass_on(*exchange(pack))
    post, sums = pl.pallas_call(
        middle_kernel,
        out_shape=(cube, lines),
        in_specs=vmem(2) + smem + vmem(4),
        out_specs=tuple(vmem(2)),
        scratch_shapes=[scratch] * 3,
        compiler_params=params,
        name="stream_collide",
    )(post, wall, neighbours, *ghosts)
    sums = spread_out(sums, "local")
    pack = pl.pallas_call(
        pack_kernel,
        out_shape=packed,
        in_specs=vmem(2),
        out_specs=vmem(1)[0],
        compiler_params=params,
        name="pack_faces",
        cost_estimate=pl.CostEstimate(flops=2000000, bytes_accessed=400000, transcendentals=0),
    )(post, wall)
    other, mate = exchange(pack)
    sums, mate = lax.optimization_barrier((sums, mate))
    plane = jnp.sum(sums[:, 0, :], axis=0, keepdims=True)
    sums = spread_out(jnp.broadcast_to(plane, (lax.axis_size("node"), LANES)), "node")
    ghosts = pass_on(other, mate)
    out = pl.pallas_call(
        last_kernel,
        out_shape=cube,
        in_specs=vmem(2) + smem + vmem(4),
        out_specs=vmem(1)[0],
        scratch_shapes=[scratch],
        compiler_params=params,
        name="stream_last",
        cost_estimate=pl.CostEstimate(flops=4000000, bytes_accessed=1000000, transcendentals=0),
    )(post, wall, neighbours, *ghosts)
    flow = jnp.sum(sums, axis=0)[:3] / (devices * BLK * BLK)
    return out.reshape(populations.shape), flow


def solution(mesh):
    in_specs = (
        P(("node", "local"), None, None),
        P(("node", "local"), None),
        P(("node", "local"), None),
    )
    out_specs = (P(("node", "local"), None, None), P())
    return jax.shard_map(shards, mesh=mesh, in_specs=in_specs, out_specs=out_specs, check_vma=False)
```

time: 303 us -> 69.6 us (0.23)
  blocking collectives: 118 us -> 0 us
  local copies, waits for them, and re-layouts: 105 us -> 2.3 us
  other arithmetic: 13.6 us -> 0.57 us
  starting transfers between devices: 45.7 us -> 53.1 us
  matrix products: 3.92 us -> 0 us
  Pallas kernels: 0 us -> 3.86 us
    psum x1 -> x0, blocking collectives: 118 us -> none  [shards(): total_momentum = lax.psum(local_momentum, ('node', 'local'))]
    another operation x130 -> x0, local copies, waits for them, and re-layouts: 38.4 us -> none  [the longest x66 27.8 us: wrap_cube(): jnp.expand_dims(sheet.reshape(blocks_here, edge_len, edge_len), 1 + dim_num)]
    all_to_all x0 -> x2, starting transfers between devices: none -> 20.4 us  [spread_out(): return lax.all_to_all(lines, axis, 0, 0, tiled=True)]
    gather x19 -> x0, local copies, waits for them, and re-layouts: 15.4 us -> none  [the longest x12 9.65 us: face_tiles(): face_sheet[:, np.array(outgoing(face_num))]]
    ppermute x12 -> x8, starting transfers between devices: 45.7 us -> 32.7 us  [swap(): return lax.ppermute(pack, ('node', 'local'), pairs)]
    squeeze x6 -> x0, local copies, waits for them, and re-layouts: 11.6 us -> none  [face_tiles(): lax.index_in_dim(cube, layer_at, axis=2 + dim_num, keepdims=False)]
    slice x14 -> x0, local copies, waits for them, and re-layouts: 10.9 us -> none  [the longest x4 6.56 us: face_tiles(): lax.index_in_dim(cube, layer_at, axis=2 + dim_num, keepdims=False)]
    gt x18 -> x0, local copies, waits for them, and re-layouts: 10.1 us -> none  [stream_cells(): source_wet > 0.5]
  transfers between devices with their start and end apart: 12 -> 10, of which waited for: 3 -> 2; matrix products, arithmetic and copies ran while one was open for 8% -> 1% of each run, Pallas kernels for 0% -> 3%
where the time goes in v1:
time: 69.6 us; the launch traced here: 69.1 us
  starting transfers between devices  53.1 us (76%)
  waiting for transfers between devices  8.47 us (12%)
  Pallas kernels  3.86 us (6%)
  local copies, waits for them, and re-layouts  2.3 us (3%)
  between operations  0.79 us (1%)
    ppermute x8, starting transfers between devices, swap(): return lax.ppermute(pack, ('node', 'local'), pairs)  32.7 us
    all_to_all x2, starting transfers between devices, spread_out(): return lax.all_to_all(lines, axis, 0, 0, tiled=True)  20.4 us
    ppermute x8, waiting for transfers between devices, swap(): return lax.ppermute(pack, ('node', 'local'), pairs)  8.46 us
    unnamed x8, local copies, waits for them, and re-layouts  1.69 us
    pallas_call x1, Pallas kernels, shards(): pl.pallas_call(middle_kernel, out_shape=(cube, lines), in_specs=vmem(2) +...  1.68 us
    pallas_call x1, Pallas kernels, shards(): pl.pallas_call(last_kernel, out_shape=cube, in_specs=vmem(2) + smem + vme...  1.57 us
  transfers between devices with their start and end apart: 10, of which 2 were waited for; matrix products, arithmetic and copies ran while one was open for 1% of the time, Pallas kernels for 3%

profile of v1, /device:TPU:1, one launch (start us, length us, event | category | flops | bytes accessed | tf_op | source)
XLA Modules:
  0.0 69.1 jit_solution(7689110765446723097)
XLA Ops:
  0.6 1.0 %copy-done = f32[1,19,4096]{2,0,1:T(1,128)S(1)} copy-done((f32[1,19,4096]{2,0,1:T(1,128)S(1)}, f32[1,19,4096]{2,0,1:T(1,128)}, u32[]{:S(2)}) %copy-start) | copy-done | bytes 311320
  1.6 0.7 %copy-done.1 = s32[1,4096]{1,0:T(1,128)S(1)} copy-done((s32[1,4096]{1,0:T(1,128)S(1)}, s32[1,4096]{1,0:T(1,128)}, u32[]{:S(2)}) %copy-start.1) | copy-done | bytes 16408
  2.3 0.4 collide_first.1
  2.7 0.0 copy-start.3
  2.7 4.0 %collective-permute-start.1 = (f32[88,128]{1,0:T(8,128)S(1)}, f32[88,128]{1,0:T(8,128)S(1)}, u32[]{:S(2)}, u32[]{:S(2)}) collective-permute-start(f32[88,128]{1,0:T(8,128)S(1)} %get-tuple-element.9), channel_id=1, source_target_pairs={{0,1},{1,0},{2,3},{3,2},{4,5},{5,4},{6,7},{7,6},{8,9},{9,8},{10,11... | collective-permute-start | bytes 135176 | tf_op jit(solution)/shard_map/ppermute | solution.py:289
  6.8 6.8 %collective-permute-start = (f32[88,128]{1,0:T(8,128)S(1)}, f32[88,128]{1,0:T(8,128)S(1)}, u32[]{:S(2)}, u32[]{:S(2)}) collective-permute-start(f32[88,128]{1,0:T(8,128)S(1)} %get-tuple-element.9), channel_id=1, source_target_pairs={{1,2},{2,1},{3,4},{4,3},{5,6},{6,5},{7,8},{8,7},{9,10},{10,9},{11,... | collective-permute-start | bytes 135176 | tf_op jit(solution)/shard_map/ppermute | solution.py:289
  13.6 3.3 %collective-permute-start.3 = (f32[88,128]{1,0:T(8,128)S(1)}, f32[88,128]{1,0:T(8,128)S(1)}, u32[]{:S(2)}, u32[]{:S(2)}) collective-permute-start(f32[88,128]{1,0:T(8,128)S(1)} %collective-permute-done.1.p1), channel_id=1, source_target_pairs={{1,2},{2,1},{3,4},{4,3},{5,6},{6,5},{7,8},{8,7},{9,10},{10,9},{11,... | collective-permute-start | bytes 135176 | tf_op jit(solution)/shard_map/ppermute | solution.py:289
  16.9 1.9 %collective-permute-start.2 = (f32[88,128]{1,0:T(8,128)S(1)}, f32[88,128]{1,0:T(8,128)S(1)}, u32[]{:S(2)}, u32[]{:S(2)}) collective-permute-start(f32[88,128]{1,0:T(8,128)S(1)} %collective-permute-done.p0), channel_id=1, source_target_pairs={{0,1},{1,0},{2,3},{3,2},{4,5},{5,4},{6,7},{7,6},{8,9},{9,8},{10,11... | collective-permute-start | bytes 135176 | tf_op jit(solution)/shard_map/ppermute | solution.py:289
  18.8 3.5 %collective-permute-done.3.p3 = f32[88,128]{1,0:T(8,128)S(1)} collective-permute-done((f32[88,128]{1,0:T(8,128)S(1)}, f32[88,128]{1,0:T(8,128)S(1)}, u32[]{:S(2)}, u32[]{:S(2)}) %collective-permute-start.3) | collective-permute-done | bytes 45088 | tf_op jit(solution)/shard_map/ppermute | solution.py:289
  22.3 1.7 %stream_collide.1 = (f32[19,32,128]{2,1,0:T(8,128)S(1)}, f32[16,8,128]{2,1,0:T(8,128)}) custom-call(f32[19,32,128]{2,1,0:T(8,128)S(1)} %get-tuple-element.8.own_ref, s32[32,128]{1,0:T(8,128)S(1)} %bitcast.6, s32[1,6]{1,0:T(1,128)S(1)} %copy-done.3, f32[88,128]{1,0:T(8,128)S(1)} %collective-permute-done.p0, f32[88,128]{1,0:T(8,128)S(1)} %collective-permute-done.1.p1, ...), custom_call_target="tpu_custom_call" | custom-call | tf_op jit(solution)/shard_map/stream_collide/pallas_call | solution.py:330
  24.0 4.9 %all-to-all-start = ((f32[16,8,128]{2,1,0:T(8,128)}), f32[16,8,128]{2,1,0:T(8,128)S(1)}, u32[]{:S(2)}, u32[]{:S(2)}) async-start(f32[16,8,128]{2,1,0:T(8,128)} %get-tuple-element.11), calls=%async_computation | async-start | bytes 131072 | tf_op jit(solution)/shard_map/all_to_all | solution.py:305
  29.0 0.2 pack_faces.1
  29.2 3.3 %collective-permute-start.5 = (f32[88,128]{1,0:T(8,128)S(1)}, f32[88,128]{1,0:T(8,128)S(1)}, u32[]{:S(2)}, u32[]{:S(2)}) collective-permute-start(f32[88,128]{1,0:T(8,128)S(1)} %pack_faces.1), channel_id=1, source_target_pairs={{0,1},{1,0},{2,3},{3,2},{4,5},{5,4},{6,7},{7,6},{8,9},{9,8},{10,11... | collective-permute-start | bytes 135176 | tf_op jit(solution)/shard_map/ppermute | solution.py:289
  32.5 7.5 %collective-permute-start.4 = (f32[88,128]{1,0:T(8,128)S(1)}, f32[88,128]{1,0:T(8,128)S(1)}, u32[]{:S(2)}, u32[]{:S(2)}) collective-permute-start(f32[88,128]{1,0:T(8,128)S(1)} %pack_faces.1), channel_id=1, source_target_pairs={{1,2},{2,1},{3,4},{4,3},{5,6},{6,5},{7,8},{8,7},{9,10},{10,9},{11,... | collective-permute-start | bytes 135176 | tf_op jit(solution)/shard_map/ppermute | solution.py:289
  39.9 0.0 collective-permute-done.5.p1
  40.0 0.6 broadcast_in_dim.2
  40.6 15.5 %all-to-all-start.1 = ((f32[32,1,128]{2,1,0:T(1,128)}), f32[32,1,128]{2,1,0:T(1,128)S(1)}, u32[]{:S(2)}, u32[]{:S(2)}) async-start(f32[32,1,128]{2,1,0:T(1,128)} %broadcast_in_dim.2), calls=%async_computation.1 | async-start | bytes 32768 | tf_op jit(solution)/shard_map/all_to_all | solution.py:305
  56.1 1.9 %collective-permute-start.6 = (f32[88,128]{1,0:T(8,128)S(1)}, f32[88,128]{1,0:T(8,128)S(1)}, u32[]{:S(2)}, u32[]{:S(2)}) collective-permute-start(f32[88,128]{1,0:T(8,128)S(1)} %collective-permute-done.4.p0), channel_id=1, source_target_pairs={{0,1},{1,0},{2,3},{3,2},{4,5},{5,4},{6,7},{7,6},{8,9},{9,8},{10,11... | collective-permute-start | bytes 135176 | tf_op jit(solution)/shard_map/ppermute | solution.py:289
  58.0 4.0 %collective-permute-start.7 = (f32[88,128]{1,0:T(8,128)S(1)}, f32[88,128]{1,0:T(8,128)S(1)}, u32[]{:S(2)}, u32[]{:S(2)}) collective-permute-start(f32[88,128]{1,0:T(8,128)S(1)} %collective-permute-done.5.p1), channel_id=1, source_target_pairs={{1,2},{2,1},{3,4},{4,3},{5,6},{6,5},{7,8},{8,7},{9,10},{10,9},{11,... | collective-permute-start | bytes 135176 | tf_op jit(solution)/shard_map/ppermute | solution.py:289
  62.0 0.0 collective-permute-done.6.p2
  62.0 5.0 %collective-permute-done.7.p3 = f32[88,128]{1,0:T(8,128)S(1)} collective-permute-done((f32[88,128]{1,0:T(8,128)S(1)}, f32[88,128]{1,0:T(8,128)S(1)}, u32[]{:S(2)}, u32[]{:S(2)}) %collective-permute-start.7) | collective-permute-done | bytes 45088 | tf_op jit(solution)/shard_map/ppermute | solution.py:289
  67.0 1.6 %stream_last.1 = f32[19,32,128]{2,1,0:T(8,128)} custom-call(f32[19,32,128]{2,1,0:T(8,128)S(1)} %get-tuple-element.10.post_ref.own_ref, s32[32,128]{1,0:T(8,128)S(1)} %bitcast.8, s32[1,6]{1,0:T(1,128)S(1)} %copy-done.3, f32[88,128]{1,0:T(8,128)S(1)} %collective-permute-done.4.p0, f32[88,128]{1,0:T(8,128)S(1)} %collective-permute-done.5.p1, ...), custom_call_target="tpu_custom_call" | custom-call | flops 4000000 | bytes 1000000 | tf_op jit(solution)/shard_map/stream_last/pallas_call | solution.py:354
  68.6 0.0 all-to-all-done.1
  68.6 0.5 slice_multiply_fusion
  (12 shorter events, 0.1 us)
Async XLA Ops:
  0.6 1.0 %copy-start = (f32[1,19,4096]{2,0,1:T(1,128)S(1)}, f32[1,19,4096]{2,0,1:T(1,128)}, u32[]{:S(2)}) copy-start(f32[1,19,4096]{2,0,1:T(1,128)} %param.3) | copy-start | bytes 933892
  1.6 0.7 %copy-start.1 = (s32[1,4096]{1,0:T(1,128)S(1)}, s32[1,4096]{1,0:T(1,128)}, u32[]{:S(2)}) copy-start(s32[1,4096]{1,0:T(1,128)} %param.4) | copy-start | bytes 49156
  2.7 19.6 %copy-start.3 = (s32[1,6]{1,0:T(1,128)S(1)}, s32[1,6]{1,0:T(1,128)}, u32[]{:S(2)}) copy-start(s32[1,6]{1,0:T(1,128)} %nb_ref.3) | copy-start | bytes 76
  2.7 10.9 %collective-permute-start.1 = (f32[88,128]{1,0:T(8,128)S(1)}, f32[88,128]{1,0:T(8,128)S(1)}, u32[]{:S(2)}, u32[]{:S(2)}) collective-permute-start(f32[88,128]{1,0:T(8,128)S(1)} %get-tuple-element.9), channel_id=1, source_target_pairs={{0,1},{1,0},{2,3},{3,2},{4,5},{5,4},{6,7},{7,6},{8,9},{9,8},{10,11... | collective-permute-start | bytes 135176 | tf_op jit(solution)/shard_map/ppermute | solution.py:289
  6.8 10.1 %collective-permute-start = (f32[88,128]{1,0:T(8,128)S(1)}, f32[88,128]{1,0:T(8,128)S(1)}, u32[]{:S(2)}, u32[]{:S(2)}) collective-permute-start(f32[88,128]{1,0:T(8,128)S(1)} %get-tuple-element.9), channel_id=1, source_target_pairs={{1,2},{2,1},{3,4},{4,3},{5,6},{6,5},{7,8},{8,7},{9,10},{10,9},{11,... | collective-permute-start | bytes 135176 | tf_op jit(solution)/shard_map/ppermute | solution.py:289
  13.6 8.7 %collective-permute-start.3 = (f32[88,128]{1,0:T(8,128)S(1)}, f32[88,128]{1,0:T(8,128)S(1)}, u32[]{:S(2)}, u32[]{:S(2)}) collective-permute-start(f32[88,128]{1,0:T(8,128)S(1)} %collective-permute-done.1.p1), channel_id=1, source_target_pairs={{1,2},{2,1},{3,4},{4,3},{5,6},{6,5},{7,8},{8,7},{9,10},{10,9},{11,... | collective-permute-start | bytes 135176 | tf_op jit(solution)/shard_map/ppermute | solution.py:289
  16.9 5.4 %collective-permute-start.2 = (f32[88,128]{1,0:T(8,128)S(1)}, f32[88,128]{1,0:T(8,128)S(1)}, u32[]{:S(2)}, u32[]{:S(2)}) collective-permute-start(f32[88,128]{1,0:T(8,128)S(1)} %collective-permute-done.p0), channel_id=1, source_target_pairs={{0,1},{1,0},{2,3},{3,2},{4,5},{5,4},{6,7},{7,6},{8,9},{9,8},{10,11... | collective-permute-start | bytes 135176 | tf_op jit(solution)/shard_map/ppermute | solution.py:289
  24.0 4.9 %copy-start.2 = (s32[1,4096]{1,0:T(1,128)S(1)}, s32[1,4096]{1,0:T(1,128)}, u32[]{:S(2)}) copy-start(s32[1,4096]{1,0:T(1,128)} %param.4) | copy-start | bytes 49156
  24.0 15.9 %all-to-all-start = ((f32[16,8,128]{2,1,0:T(8,128)}), f32[16,8,128]{2,1,0:T(8,128)S(1)}, u32[]{:S(2)}, u32[]{:S(2)}) async-start(f32[16,8,128]{2,1,0:T(8,128)} %get-tuple-element.11), calls=%async_computation | async-start | bytes 131072 | tf_op jit(solution)/shard_map/all_to_all | solution.py:305
  29.2 10.8 %collective-permute-start.5 = (f32[88,128]{1,0:T(8,128)S(1)}, f32[88,128]{1,0:T(8,128)S(1)}, u32[]{:S(2)}, u32[]{:S(2)}) collective-permute-start(f32[88,128]{1,0:T(8,128)S(1)} %pack_faces.1), channel_id=1, source_target_pairs={{0,1},{1,0},{2,3},{3,2},{4,5},{5,4},{6,7},{7,6},{8,9},{9,8},{10,11... | collective-permute-start | bytes 135176 | tf_op jit(solution)/shard_map/ppermute | solution.py:289
  32.5 23.6 %collective-permute-start.4 = (f32[88,128]{1,0:T(8,128)S(1)}, f32[88,128]{1,0:T(8,128)S(1)}, u32[]{:S(2)}, u32[]{:S(2)}) collective-permute-start(f32[88,128]{1,0:T(8,128)S(1)} %pack_faces.1), channel_id=1, source_target_pairs={{1,2},{2,1},{3,4},{4,3},{5,6},{6,5},{7,8},{8,7},{9,10},{10,9},{11,... | collective-permute-start | bytes 135176 | tf_op jit(solution)/shard_map/ppermute | solution.py:289
  40.6 28.0 %all-to-all-start.1 = ((f32[32,1,128]{2,1,0:T(1,128)}), f32[32,1,128]{2,1,0:T(1,128)S(1)}, u32[]{:S(2)}, u32[]{:S(2)}) async-start(f32[32,1,128]{2,1,0:T(1,128)} %broadcast_in_dim.2), calls=%async_computation.1 | async-start | bytes 32768 | tf_op jit(solution)/shard_map/all_to_all | solution.py:305
  56.1 5.9 %collective-permute-start.6 = (f32[88,128]{1,0:T(8,128)S(1)}, f32[88,128]{1,0:T(8,128)S(1)}, u32[]{:S(2)}, u32[]{:S(2)}) collective-permute-start(f32[88,128]{1,0:T(8,128)S(1)} %collective-permute-done.4.p0), channel_id=1, source_target_pairs={{0,1},{1,0},{2,3},{3,2},{4,5},{5,4},{6,7},{7,6},{8,9},{9,8},{10,11... | collective-permute-start | bytes 135176 | tf_op jit(solution)/shard_map/ppermute | solution.py:289
  58.0 9.0 %collective-permute-start.7 = (f32[88,128]{1,0:T(8,128)S(1)}, f32[88,128]{1,0:T(8,128)S(1)}, u32[]{:S(2)}, u32[]{:S(2)}) collective-permute-start(f32[88,128]{1,0:T(8,128)S(1)} %collective-permute-done.5.p1), channel_id=1, source_target_pairs={{1,2},{2,1},{3,4},{4,3},{5,6},{6,5},{7,8},{8,7},{9,10},{10,9},{11,... | collective-permute-start | bytes 135176 | tf_op jit(solution)/shard_map/ppermute | solution.py:289

commit v2 on v1

--- a/solution.py
+++ b/solution.py
@@ -269,8 +269,13 @@
     sum_ref[...] = line
 
 
-def last_kernel(own_ref, fluid_ref, nb_ref, p0, p1, p2, p3, out_ref, work_ref):
+def last_kernel(own_ref, fluid_ref, nb_ref, p0, p1, p3, p2, sum_ref, out_ref, flow_ref, work_ref):
     grid = Grid()
+    total = jnp.sum(sum_ref[...], axis=0, keepdims=True)
+    lane = lax.broadcasted_iota(jnp.int32, (1, LANES), 1)
+    cells = lax.axis_size("node") * lax.axis_size("local") * BLK * BLK
+    for dim in range(3):
+        flow_ref[dim] = jnp.sum(jnp.where(lane == dim, total, 0.0)) / cells
     wet = fluid_ref[...] > 0
 
     def put(i, value, open_link):
@@ -309,10 +314,9 @@
     f32 = jnp.float32
     cube = jax.ShapeDtypeStruct((19, ROWS, LANES), f32)
     packed = jax.ShapeDtypeStruct((PACK_ROWS, LANES), f32)
-    lines = jax.ShapeDtypeStruct((lax.axis_size("local"), 8, LANES), f32)
+    lines = jax.ShapeDtypeStruct((lax.axis_size("local"), 4, LANES), f32)
     scratch = pltpu.VMEM((19, ROWS, LANES), f32)
     smem = [pl.BlockSpec(memory_space=pltpu.SMEM)]
-    devices = lax.axis_size("node") * lax.axis_size("local")
     params = pltpu.CompilerParams(vmem_limit_bytes=16 * 2**20)
     pop = populations.reshape(19, ROWS, LANES)
     wall = fluid.reshape(ROWS, LANES)
@@ -350,18 +354,17 @@
     sums, mate = lax.optimization_barrier((sums, mate))
     plane = jnp.sum(sums[:, 0, :], axis=0, keepdims=True)
     sums = spread_out(jnp.broadcast_to(plane, (lax.axis_size("node"), LANES)), "node")
-    ghosts = pass_on(other, mate)
-    out = pl.pallas_call(
+    other, mate, past_mate, past_other = pass_on(other, mate)
+    out, flow = pl.pallas_call(
         last_kernel,
-        out_shape=cube,
-        in_specs=vmem(2) + smem + vmem(4),
-        out_specs=vmem(1)[0],
+        out_shape=(cube, jax.ShapeDtypeStruct((3,), f32)),
+        in_specs=vmem(2) + smem + vmem(5),
+        out_specs=tuple(vmem(1) + smem),
         scratch_shapes=[scratch],
         compiler_params=params,
         name="stream_last",
         cost_estimate=pl.CostEstimate(flops=4000000, bytes_accessed=1000000, transcendentals=0),
-    )(post, wall, neighbours, *ghosts)
-    flow = jnp.sum(sums, axis=0)[:3] / (devices * BLK * BLK)
+    )(post, wall, neighbours, other, mate, past_other, past_mate, sums)
     return out.reshape(populations.shape), flow
 
 

time: 69.6 us -> 71.1 us (1.022)
  waiting for transfers between devices: 8.47 us -> 9.75 us
  starting transfers between devices: 53.1 us -> 53.9 us
    all_to_all x2, waiting for transfers between devices: 0.01 us -> 2.74 us  [spread_out(): return lax.all_to_all(lines, axis, 0, 0, tiled=True)]
    all_to_all x2, starting transfers between devices: 20.4 us -> 21.9 us  [spread_out(): return lax.all_to_all(lines, axis, 0, 0, tiled=True)]
    ppermute x8, waiting for transfers between devices: 8.46 us -> 7.01 us  [swap(): return lax.ppermute(pack, ('node', 'local'), pairs)]
    ppermute x8, starting transfers between devices: 32.7 us -> 31.9 us  [swap(): return lax.ppermute(pack, ('node', 'local'), pairs)]
  transfers between devices with their start and end apart: 10 -> 10, of which waited for: 2 -> 3; matrix products, arithmetic and copies ran while one was open for 1% -> 1% of each run, Pallas kernels for 3% -> 0%
where the time goes in v2:
time: 71.1 us; the launch traced here: 70.6 us
  starting transfers between devices  53.9 us (76%)
  waiting for transfers between devices  9.75 us (14%)
  Pallas kernels  3.87 us (5%)
  local copies, waits for them, and re-layouts  2.3 us (3%)
  between operations  0.78 us (1%)
    ppermute x8, starting transfers between devices, swap(): return lax.ppermute(pack, ('node', 'local'), pairs)  31.9 us
    all_to_all x2, starting transfers between devices, spread_out(): return lax.all_to_all(lines, axis, 0, 0, tiled=True)  21.9 us
    ppermute x8, waiting for transfers between devices, swap(): return lax.ppermute(pack, ('node', 'local'), pairs)  7.01 us
    all_to_all x2, waiting for transfers between devices, spread_out(): return lax.all_to_all(lines, axis, 0, 0, tiled=True)  2.74 us
    unnamed x8, local copies, waits for them, and re-layouts  1.69 us
    pallas_call x1, Pallas kernels, shards(): pl.pallas_call(middle_kernel, out_shape=(cube, lines), in_specs=vmem(2) +...  1.67 us
    pallas_call x1, Pallas kernels, shards(): pl.pallas_call(last_kernel, out_shape=(cube, jax.ShapeDtypeStruct((3,), f...  1.59 us
  transfers between devices with their start and end apart: 10, of which 3 were waited for; matrix products, arithmetic and copies ran while one was open for 1% of the time, Pallas kernels for 0%

profile of v2, /device:TPU:1, one launch (start us, length us, event | category | flops | bytes accessed | tf_op | source)
XLA Modules:
  0.0 70.6 jit_solution(2688228772461454221)
XLA Ops:
  0.6 1.0 %copy-done = f32[1,19,4096]{2,0,1:T(1,128)S(1)} copy-done((f32[1,19,4096]{2,0,1:T(1,128)S(1)}, f32[1,19,4096]{2,0,1:T(1,128)}, u32[]{:S(2)}) %copy-start) | copy-done | bytes 311320
  1.6 0.7 %copy-done.1 = s32[1,4096]{1,0:T(1,128)S(1)} copy-done((s32[1,4096]{1,0:T(1,128)S(1)}, s32[1,4096]{1,0:T(1,128)}, u32[]{:S(2)}) %copy-start.1) | copy-done | bytes 16408
  2.3 0.4 collide_first.1
  2.7 0.0 copy-start.3
  2.7 4.0 %collective-permute-start.1 = (f32[88,128]{1,0:T(8,128)S(1)}, f32[88,128]{1,0:T(8,128)S(1)}, u32[]{:S(2)}, u32[]{:S(2)}) collective-permute-start(f32[88,128]{1,0:T(8,128)S(1)} %get-tuple-element.11), channel_id=1, source_target_pairs={{0,1},{1,0},{2,3},{3,2},{4,5},{5,4},{6,7},{7,6},{8,9},{9,8},{10,11... | collective-permute-start | bytes 135176 | tf_op jit(solution)/shard_map/ppermute | solution.py:294
  6.8 6.8 %collective-permute-start = (f32[88,128]{1,0:T(8,128)S(1)}, f32[88,128]{1,0:T(8,128)S(1)}, u32[]{:S(2)}, u32[]{:S(2)}) collective-permute-start(f32[88,128]{1,0:T(8,128)S(1)} %get-tuple-element.11), channel_id=1, source_target_pairs={{1,2},{2,1},{3,4},{4,3},{5,6},{6,5},{7,8},{8,7},{9,10},{10,9},{11,... | collective-permute-start | bytes 135176 | tf_op jit(solution)/shard_map/ppermute | solution.py:294
  13.6 3.3 %collective-permute-start.3 = (f32[88,128]{1,0:T(8,128)S(1)}, f32[88,128]{1,0:T(8,128)S(1)}, u32[]{:S(2)}, u32[]{:S(2)}) collective-permute-start(f32[88,128]{1,0:T(8,128)S(1)} %collective-permute-done.1.p1), channel_id=1, source_target_pairs={{1,2},{2,1},{3,4},{4,3},{5,6},{6,5},{7,8},{8,7},{9,10},{10,9},{11,... | collective-permute-start | bytes 135176 | tf_op jit(solution)/shard_map/ppermute | solution.py:294
  16.9 1.9 %collective-permute-start.2 = (f32[88,128]{1,0:T(8,128)S(1)}, f32[88,128]{1,0:T(8,128)S(1)}, u32[]{:S(2)}, u32[]{:S(2)}) collective-permute-start(f32[88,128]{1,0:T(8,128)S(1)} %collective-permute-done.p0), channel_id=1, source_target_pairs={{0,1},{1,0},{2,3},{3,2},{4,5},{5,4},{6,7},{7,6},{8,9},{9,8},{10,11... | collective-permute-start | bytes 135176 | tf_op jit(solution)/shard_map/ppermute | solution.py:294
  18.8 3.5 %collective-permute-done.3.p3 = f32[88,128]{1,0:T(8,128)S(1)} collective-permute-done((f32[88,128]{1,0:T(8,128)S(1)}, f32[88,128]{1,0:T(8,128)S(1)}, u32[]{:S(2)}, u32[]{:S(2)}) %collective-permute-start.3) | collective-permute-done | bytes 45088 | tf_op jit(solution)/shard_map/ppermute | solution.py:294
  22.3 1.7 %stream_collide.1 = (f32[19,32,128]{2,1,0:T(8,128)S(1)}, f32[16,4,128]{2,1,0:T(4,128)}) custom-call(f32[19,32,128]{2,1,0:T(8,128)S(1)} %get-tuple-element.10.own_ref, s32[32,128]{1,0:T(8,128)S(1)} %bitcast.6, s32[1,6]{1,0:T(1,128)S(1)} %copy-done.3, f32[88,128]{1,0:T(8,128)S(1)} %collective-permute-done.p0, f32[88,128]{1,0:T(8,128)S(1)} %collective-permute-done.1.p1, ...), custom_call_target="tpu_custom_call" | custom-call | tf_op jit(solution)/shard_map/stream_collide/pallas_call | solution.py:334
  24.0 0.2 pack_faces.1
  24.2 1.9 %collective-permute-start.5 = (f32[88,128]{1,0:T(8,128)S(1)}, f32[88,128]{1,0:T(8,128)S(1)}, u32[]{:S(2)}, u32[]{:S(2)}) collective-permute-start(f32[88,128]{1,0:T(8,128)S(1)} %pack_faces.1), channel_id=1, source_target_pairs={{0,1},{1,0},{2,3},{3,2},{4,5},{5,4},{6,7},{7,6},{8,9},{9,8},{10,11... | collective-permute-start | bytes 135176 | tf_op jit(solution)/shard_map/ppermute | solution.py:294
  26.1 5.7 %all-to-all-start = ((f32[16,4,128]{2,1,0:T(4,128)}), f32[16,4,128]{2,1,0:T(4,128)S(1)}, u32[]{:S(2)}, u32[]{:S(2)}) async-start(f32[16,4,128]{2,1,0:T(4,128)} %get-tuple-element.13), calls=%async_computation | async-start | bytes 65536 | tf_op jit(solution)/shard_map/all_to_all | solution.py:310
  31.9 8.5 %collective-permute-start.4 = (f32[88,128]{1,0:T(8,128)S(1)}, f32[88,128]{1,0:T(8,128)S(1)}, u32[]{:S(2)}, u32[]{:S(2)}) collective-permute-start(f32[88,128]{1,0:T(8,128)S(1)} %pack_faces.1), channel_id=1, source_target_pairs={{1,2},{2,1},{3,4},{4,3},{5,6},{6,5},{7,8},{8,7},{9,10},{10,9},{11,... | collective-permute-start | bytes 135176 | tf_op jit(solution)/shard_map/ppermute | solution.py:294
  40.4 0.0 all-to-all-done
  40.4 0.0 collective-permute-done.5.p1
  40.4 0.6 broadcast_in_dim.2
  41.1 16.2 %all-to-all-start.1 = ((f32[32,1,128]{2,1,0:T(1,128)}), f32[32,1,128]{2,1,0:T(1,128)S(1)}, u32[]{:S(2)}, u32[]{:S(2)}) async-start(f32[32,1,128]{2,1,0:T(1,128)} %broadcast_in_dim.2), calls=%async_computation.1 | async-start | bytes 32768 | tf_op jit(solution)/shard_map/all_to_all | solution.py:310
  57.3 3.5 %collective-permute-start.6 = (f32[88,128]{1,0:T(8,128)S(1)}, f32[88,128]{1,0:T(8,128)S(1)}, u32[]{:S(2)}, u32[]{:S(2)}) collective-permute-start(f32[88,128]{1,0:T(8,128)S(1)} %collective-permute-done.5.p1), channel_id=1, source_target_pairs={{1,2},{2,1},{3,4},{4,3},{5,6},{6,5},{7,8},{8,7},{9,10},{10,9},{11,... | collective-permute-start | bytes 135176 | tf_op jit(solution)/shard_map/ppermute | solution.py:294
  60.8 1.9 %collective-permute-start.7 = (f32[88,128]{1,0:T(8,128)S(1)}, f32[88,128]{1,0:T(8,128)S(1)}, u32[]{:S(2)}, u32[]{:S(2)}) collective-permute-start(f32[88,128]{1,0:T(8,128)S(1)} %collective-permute-done.4.p0), channel_id=1, source_target_pairs={{0,1},{1,0},{2,3},{3,2},{4,5},{5,4},{6,7},{7,6},{8,9},{9,8},{10,11... | collective-permute-start | bytes 135176 | tf_op jit(solution)/shard_map/ppermute | solution.py:294
  62.8 3.5 %collective-permute-done.6.p3 = f32[88,128]{1,0:T(8,128)S(1)} collective-permute-done((f32[88,128]{1,0:T(8,128)S(1)}, f32[88,128]{1,0:T(8,128)S(1)}, u32[]{:S(2)}, u32[]{:S(2)}) %collective-permute-start.6) | collective-permute-done | bytes 45088 | tf_op jit(solution)/shard_map/ppermute | solution.py:294
  66.3 0.0 collective-permute-done.7.p2
  66.3 2.7 %all-to-all-done.1 = f32[32,1,128]{2,1,0:T(1,128)S(1)} async-done(((f32[32,1,128]{2,1,0:T(1,128)}), f32[32,1,128]{2,1,0:T(1,128)S(1)}, u32[]{:S(2)}, u32[]{:S(2)}) %all-to-all-start.1) | async-done | bytes 16416 | tf_op jit(solution)/shard_map/all_to_all | solution.py:310
  69.0 1.6 %stream_last.1 = (f32[19,32,128]{2,1,0:T(8,128)}, f32[3]{0:T(128)}) custom-call(f32[19,32,128]{2,1,0:T(8,128)S(1)} %get-tuple-element.12.post_ref.own_ref, s32[32,128]{1,0:T(8,128)S(1)} %bitcast.8, s32[1,6]{1,0:T(1,128)S(1)} %copy-done.3, f32[88,128]{1,0:T(8,128)S(1)} %collective-permute-done.4.p0, f32[88,128]{1,0:T(8,128)S(1)} %collective-permute-done.5.p1, ...), custom_call_target="tpu_custom_call" | custom-call | flops 4000000 | bytes 1000000 | tf_op jit(solution)/shard_map/stream_last/pallas_call | solution.py:358
  (10 shorter events, 0.1 us)
Async XLA Ops:
  0.6 1.0 %copy-start = (f32[1,19,4096]{2,0,1:T(1,128)S(1)}, f32[1,19,4096]{2,0,1:T(1,128)}, u32[]{:S(2)}) copy-start(f32[1,19,4096]{2,0,1:T(1,128)} %param.3) | copy-start | bytes 933892
  1.6 0.7 %copy-start.1 = (s32[1,4096]{1,0:T(1,128)S(1)}, s32[1,4096]{1,0:T(1,128)}, u32[]{:S(2)}) copy-start(s32[1,4096]{1,0:T(1,128)} %param.4) | copy-start | bytes 49156
  2.7 19.6 %copy-start.3 = (s32[1,6]{1,0:T(1,128)S(1)}, s32[1,6]{1,0:T(1,128)}, u32[]{:S(2)}) copy-start(s32[1,6]{1,0:T(1,128)} %nb_ref.3) | copy-start | bytes 76
  2.7 10.9 %collective-permute-start.1 = (f32[88,128]{1,0:T(8,128)S(1)}, f32[88,128]{1,0:T(8,128)S(1)}, u32[]{:S(2)}, u32[]{:S(2)}) collective-permute-start(f32[88,128]{1,0:T(8,128)S(1)} %get-tuple-element.11), channel_id=1, source_target_pairs={{0,1},{1,0},{2,3},{3,2},{4,5},{5,4},{6,7},{7,6},{8,9},{9,8},{10,11... | collective-permute-start | bytes 135176 | tf_op jit(solution)/shard_map/ppermute | solution.py:294
  6.8 10.1 %collective-permute-start = (f32[88,128]{1,0:T(8,128)S(1)}, f32[88,128]{1,0:T(8,128)S(1)}, u32[]{:S(2)}, u32[]{:S(2)}) collective-permute-start(f32[88,128]{1,0:T(8,128)S(1)} %get-tuple-element.11), channel_id=1, source_target_pairs={{1,2},{2,1},{3,4},{4,3},{5,6},{6,5},{7,8},{8,7},{9,10},{10,9},{11,... | collective-permute-start | bytes 135176 | tf_op jit(solution)/shard_map/ppermute | solution.py:294
  13.6 8.7 %collective-permute-start.3 = (f32[88,128]{1,0:T(8,128)S(1)}, f32[88,128]{1,0:T(8,128)S(1)}, u32[]{:S(2)}, u32[]{:S(2)}) collective-permute-start(f32[88,128]{1,0:T(8,128)S(1)} %collective-permute-done.1.p1), channel_id=1, source_target_pairs={{1,2},{2,1},{3,4},{4,3},{5,6},{6,5},{7,8},{8,7},{9,10},{10,9},{11,... | collective-permute-start | bytes 135176 | tf_op jit(solution)/shard_map/ppermute | solution.py:294
  16.9 5.4 %collective-permute-start.2 = (f32[88,128]{1,0:T(8,128)S(1)}, f32[88,128]{1,0:T(8,128)S(1)}, u32[]{:S(2)}, u32[]{:S(2)}) collective-permute-start(f32[88,128]{1,0:T(8,128)S(1)} %collective-permute-done.p0), channel_id=1, source_target_pairs={{0,1},{1,0},{2,3},{3,2},{4,5},{5,4},{6,7},{7,6},{8,9},{9,8},{10,11... | collective-permute-start | bytes 135176 | tf_op jit(solution)/shard_map/ppermute | solution.py:294
  24.2 16.2 %collective-permute-start.5 = (f32[88,128]{1,0:T(8,128)S(1)}, f32[88,128]{1,0:T(8,128)S(1)}, u32[]{:S(2)}, u32[]{:S(2)}) collective-permute-start(f32[88,128]{1,0:T(8,128)S(1)} %pack_faces.1), channel_id=1, source_target_pairs={{0,1},{1,0},{2,3},{3,2},{4,5},{5,4},{6,7},{7,6},{8,9},{9,8},{10,11... | collective-permute-start | bytes 135176 | tf_op jit(solution)/shard_map/ppermute | solution.py:294
  26.1 14.3 %all-to-all-start = ((f32[16,4,128]{2,1,0:T(4,128)}), f32[16,4,128]{2,1,0:T(4,128)S(1)}, u32[]{:S(2)}, u32[]{:S(2)}) async-start(f32[16,4,128]{2,1,0:T(4,128)} %get-tuple-element.13), calls=%async_computation | async-start | bytes 65536 | tf_op jit(solution)/shard_map/all_to_all | solution.py:310
  31.9 29.0 %collective-permute-start.4 = (f32[88,128]{1,0:T(8,128)S(1)}, f32[88,128]{1,0:T(8,128)S(1)}, u32[]{:S(2)}, u32[]{:S(2)}) collective-permute-start(f32[88,128]{1,0:T(8,128)S(1)} %pack_faces.1), channel_id=1, source_target_pairs={{1,2},{2,1},{3,4},{4,3},{5,6},{6,5},{7,8},{8,7},{9,10},{10,9},{11,... | collective-permute-start | bytes 135176 | tf_op jit(solution)/shard_map/ppermute | solution.py:294
  41.1 27.9 %copy-start.2 = (s32[1,4096]{1,0:T(1,128)S(1)}, s32[1,4096]{1,0:T(1,128)}, u32[]{:S(2)}) copy-start(s32[1,4096]{1,0:T(1,128)} %param.4) | copy-start | bytes 49156
  41.1 27.9 %all-to-all-start.1 = ((f32[32,1,128]{2,1,0:T(1,128)}), f32[32,1,128]{2,1,0:T(1,128)S(1)}, u32[]{:S(2)}, u32[]{:S(2)}) async-start(f32[32,1,128]{2,1,0:T(1,128)} %broadcast_in_dim.2), calls=%async_computation.1 | async-start | bytes 32768 | tf_op jit(solution)/shard_map/all_to_all | solution.py:310
  57.3 9.0 %collective-permute-start.6 = (f32[88,128]{1,0:T(8,128)S(1)}, f32[88,128]{1,0:T(8,128)S(1)}, u32[]{:S(2)}, u32[]{:S(2)}) collective-permute-start(f32[88,128]{1,0:T(8,128)S(1)} %collective-permute-done.5.p1), channel_id=1, source_target_pairs={{1,2},{2,1},{3,4},{4,3},{5,6},{6,5},{7,8},{8,7},{9,10},{10,9},{11,... | collective-permute-start | bytes 135176 | tf_op jit(solution)/shard_map/ppermute | solution.py:294
  60.8 5.4 %collective-permute-start.7 = (f32[88,128]{1,0:T(8,128)S(1)}, f32[88,128]{1,0:T(8,128)S(1)}, u32[]{:S(2)}, u32[]{:S(2)}) collective-permute-start(f32[88,128]{1,0:T(8,128)S(1)} %collective-permute-done.4.p0), channel_id=1, source_target_pairs={{0,1},{1,0},{2,3},{3,2},{4,5},{5,4},{6,7},{7,6},{8,9},{9,8},{10,11... | collective-permute-start | bytes 135176 | tf_op jit(solution)/shard_map/ppermute | solution.py:294

commit v3 on v1

--- a/solution.py
+++ b/solution.py
@@ -163,20 +163,29 @@
     return ((me + 1) ^ 1) - 1
 
 
-def pull(grid, wet, own_ref, nb_ref, pack_refs, work_ref, put):
-    me = lax.axis_index("node") * lax.axis_size("local") + lax.axis_index("local")
-    sources = [other_side(me), pair_mate(me), other_side(pair_mate(me)), pair_mate(other_side(me))]
-
+def place():
+    return lax.axis_index("node") * lax.axis_size("local") + lax.axis_index("local")
+
+
+def pick(grid, nb_ref, tiles, base_ref=None):
     def select(face, start, rows):
         block = nb_ref[0, face]
-        value = jnp.zeros((rows, LANES), jnp.float32)
-        for source, ref in zip(sources, pack_refs):
+        if base_ref is None:
+            value = jnp.zeros((rows, LANES), jnp.float32)
+        else:
+            value = base_ref[start : start + rows, :]
+        for source, ref in tiles:
             value = jnp.where((block >= 0) & (block == source), ref[start : start + rows, :], value)
         return value
 
     ghost_y = jnp.where(grid.odd, select(2, Y_AT, ROWS), select(3, Y_AT, ROWS))
     ghost_z = jnp.where(grid.z >= 8, select(4, Z_AT, ROWS), select(5, Z_AT, ROWS))
-    ghost_x = {1: select(0, X_HIGH_AT, 12), -1: select(1, X_LOW_AT, 12)}
+    return ghost_y, ghost_z, select(0, X_HIGH_AT, 12), select(1, X_LOW_AT, 12)
+
+
+def pull(grid, wet, own_ref, nb_ref, tiles, base_ref, work_ref, put):
+    ghost_y, ghost_z, low_x, high_x = pick(grid, nb_ref, tiles, base_ref)
+    ghost_x = {1: low_x, -1: high_x}
     wet_y = {
         1: lane_roll(ghost_y, 112 - 16 * WET_SLOT) > 0.5,
         -1: lane_roll(ghost_y, -16 * WET_SLOT) > 0.5,
@@ -234,12 +243,7 @@
     write_pack(grid, g, wet, pack_ref)
 
 
-def pack_kernel(post_ref, fluid_ref, pack_ref):
-    wet = fluid_ref[...] > 0
-    write_pack(Grid(), [jnp.where(wet, post_ref[i], 0.0) for i in range(19)], wet, pack_ref)
-
-
-def middle_kernel(own_ref, fluid_ref, nb_ref, p0, p1, p2, p3, post_ref, sum_ref, work_ref, now_ref, sign_ref):
+def middle_kernel(own_ref, fluid_ref, nb_ref, p0, p1, p2, p3, post_ref, pack_ref, sum_hbm, work_ref, now_ref, sign_ref, sum_ref, sem):
     grid = Grid()
     wet = fluid_ref[...] > 0
 
@@ -248,10 +252,15 @@
         if i:
             sign_ref[i] = jnp.where(wet, jnp.where(open_link, 1.0, -1.0), 0.0)
 
-    pull(grid, wet, own_ref, nb_ref, (p0, p1, p2, p3), work_ref, put)
+    me = place()
+    tiles = (
+        (other_side(me), p0),
+        (pair_mate(me), p1),
+        (other_side(pair_mate(me)), p2),
+        (pair_mate(other_side(me)), p3),
+    )
+    pull(grid, wet, own_ref, nb_ref, tiles, None, work_ref, put)
     g = collide([now_ref[i] for i in range(19)], wet)
-    for i in range(19):
-        post_ref[i] = jnp.where(wet, g[i], BIG)
     totals = [None] * 3
     for i in range(1, 19, 2):
         signed = (g[i] * sign_ref[i + 1] - g[i + 1] * sign_ref[i]) * WEIGHTS[i]
@@ -267,16 +276,32 @@
         total = jnp.sum(jnp.sum(totals[dim], axis=0, keepdims=True), axis=1, keepdims=True)[None]
         line = jnp.where(lane == dim, total, line)
     sum_ref[...] = line
-
-
-def last_kernel(own_ref, fluid_ref, nb_ref, p0, p1, p2, p3, out_ref, work_ref):
+    sum_copy = pltpu.make_async_copy(sum_ref, sum_hbm, sem)
+    sum_copy.start()
+    for i in range(19):
+        post_ref[i] = jnp.where(wet, g[i], BIG)
+    write_pack(grid, g, wet, pack_ref)
+    sum_copy.wait()
+
+
+def pick_kernel(nb_ref, p0, p1, p3, tile_ref):
+    me = place()
+    tiles = ((other_side(me), p0), (pair_mate(me), p1), (pair_mate(other_side(me)), p3))
+    ghost_y, ghost_z, low_x, high_x = pick(Grid(), nb_ref, tiles)
+    tile_ref[Y_AT : Y_AT + ROWS, :] = ghost_y
+    tile_ref[Z_AT : Z_AT + ROWS, :] = ghost_z
+    tile_ref[X_HIGH_AT : X_HIGH_AT + 12, :] = low_x
+    tile_ref[X_LOW_AT : X_LOW_AT + 12, :] = high_x
+
+
+def last_kernel(own_ref, fluid_ref, nb_ref, base_ref, p2, out_ref, work_ref):
     grid = Grid()
     wet = fluid_ref[...] > 0
 
     def put(i, value, open_link):
         out_ref[i] = value
 
-    pull(grid, wet, own_ref, nb_ref, (p0, p1, p2, p3), work_ref, put)
+    pull(grid, wet, own_ref, nb_ref, ((other_side(pair_mate(place())), p2),), base_ref, work_ref, put)
 
 
 def vmem(count):
@@ -323,44 +348,44 @@
         in_specs=[pl.BlockSpec(memory_space=pltpu.HBM)] * 2,
         out_specs=tuple(vmem(2)),
         scratch_shapes=[scratch, pltpu.VMEM((ROWS, LANES), jnp.int32), pltpu.SemaphoreType.DMA((2,))],
-        compiler_params=params,
+        compiler_params=pltpu.CompilerParams(vmem_limit_bytes=60 * 2**20),
         name="collide_first",
     )(pop, wall)
     ghosts = pass_on(*exchange(pack))
-    post, sums = pl.pallas_call(
+    post, pack, sums = pl.pallas_call(
         middle_kernel,
-        out_shape=(cube, lines),
+        out_shape=(cube, packed, lines),
         in_specs=vmem(2) + smem + vmem(4),
-        out_specs=tuple(vmem(2)),
-        scratch_shapes=[scratch] * 3,
+        out_specs=tuple(vmem(2)) + (pl.BlockSpec(memory_space=pl.ANY),),
+        scratch_shapes=[scratch] * 3 + [pltpu.VMEM(lines.shape, f32), pltpu.SemaphoreType.DMA],
         compiler_params=params,
         name="stream_collide",
     )(post, wall, neighbours, *ghosts)
     sums = spread_out(sums, "local")
-    pack = pl.pallas_call(
-        pack_kernel,
-        out_shape=packed,
-        in_specs=vmem(2),
-        out_specs=vmem(1)[0],
-        compiler_params=params,
-        name="pack_faces",
-        cost_estimate=pl.CostEstimate(flops=2000000, bytes_accessed=400000, transcendentals=0),
-    )(post, wall)
     other, mate = exchange(pack)
     sums, mate = lax.optimization_barrier((sums, mate))
     plane = jnp.sum(sums[:, 0, :], axis=0, keepdims=True)
     sums = spread_out(jnp.broadcast_to(plane, (lax.axis_size("node"), LANES)), "node")
-    ghosts = pass_on(other, mate)
+    other, mate, past_mate, past_other = pass_on(other, mate)
+    tile = pl.pallas_call(
+        pick_kernel,
+        out_shape=packed,
+        in_specs=smem + vmem(3),
+        out_specs=vmem(1)[0],
+        compiler_params=params,
+        name="pick_tiles",
+        cost_estimate=pl.CostEstimate(flops=1000000, bytes_accessed=400000, transcendentals=0),
+    )(neighbours, other, mate, past_other)
     out = pl.pallas_call(
         last_kernel,
         out_shape=cube,
-        in_specs=vmem(2) + smem + vmem(4),
+        in_specs=vmem(2) + smem + vmem(2),
         out_specs=vmem(1)[0],
         scratch_shapes=[scratch],
         compiler_params=params,
         name="stream_last",
         cost_estimate=pl.CostEstimate(flops=4000000, bytes_accessed=1000000, transcendentals=0),
-    )(post, wall, neighbours, *ghosts)
+    )(post, wall, neighbours, tile, past_mate)
     flow = jnp.sum(sums, axis=0)[:3] / (devices * BLK * BLK)
     return out.reshape(populations.shape), flow
 

time: 69.6 us -> 69.4 us (level)
  Pallas kernels: 3.86 us -> 5.79 us
  waiting for transfers between devices: 8.47 us -> 7.67 us
  local copies, waits for them, and re-layouts: 2.3 us -> 1.59 us
    pallas_call x1, Pallas kernels: 0.4 us -> 1.89 us  [shards(): pl.pallas_call(first_kernel, out_shape=(cube, packed), in_specs=[pl.Block...]
    ppermute x8, waiting for transfers between devices: 8.46 us -> 7.07 us  [swap(): return lax.ppermute(pack, ('node', 'local'), pairs)]
    unnamed x8 -> x6, local copies, waits for them, and re-layouts: 1.69 us -> 0.97 us
  transfers between devices with their start and end apart: 10 -> 10, of which waited for: 2 -> 3; matrix products, arithmetic and copies ran while one was open for 1% -> 1% of each run, Pallas kernels for 3% -> 3%
where the time goes in v3:
time: 69.4 us; the launch traced here: 68.9 us
  starting transfers between devices  52.5 us (76%)
  waiting for transfers between devices  7.67 us (11%)
  Pallas kernels  5.79 us (8%)
  local copies, waits for them, and re-layouts  1.59 us (2%)
  between operations  0.81 us (1%)
    ppermute x8, starting transfers between devices, swap(): return lax.ppermute(pack, ('node', 'local'), pairs)  32.2 us
    all_to_all x2, starting transfers between devices, spread_out(): return lax.all_to_all(lines, axis, 0, 0, tiled=True)  20.3 us
    ppermute x8, waiting for transfers between devices, swap(): return lax.ppermute(pack, ('node', 'local'), pairs)  7.07 us
    pallas_call x1, Pallas kernels, shards(): pl.pallas_call(first_kernel, out_shape=(cube, packed), in_specs=[pl.Block...  1.89 us
    pallas_call x1, Pallas kernels, shards(): pl.pallas_call(middle_kernel, out_shape=(cube, packed, lines), in_specs=v...  1.76 us
    pallas_call x1, Pallas kernels, shards(): pl.pallas_call(last_kernel, out_shape=cube, in_specs=vmem(2) + smem + vme...  1.56 us
  transfers between devices with their start and end apart: 10, of which 3 were waited for; matrix products, arithmetic and copies ran while one was open for 1% of the time, Pallas kernels for 3%

profile of v3, /device:TPU:1, one launch (start us, length us, event | category | flops | bytes accessed | tf_op | source)
XLA Modules:
  0.0 68.9 jit_solution(15991557202283260081)
XLA Ops:
  0.6 1.9 %collide_first.1 = (f32[19,32,128]{2,1,0:T(8,128)}, f32[88,128]{1,0:T(8,128)}) custom-call(f32[19,32,128]{2,1,0:T(8,128)} %bitcast.7, s32[32,128]{1,0:T(8,128)} %bitcast.4), custom_call_target="tpu_custom_call" | custom-call | tf_op jit(solution)/shard_map/collide_first/pallas_call | solution.py:345
  2.5 0.0 copy-start.2
  2.6 4.0 %collective-permute-start.1 = (f32[88,128]{1,0:T(8,128)}, f32[88,128]{1,0:T(8,128)S(1)}, u32[]{:S(2)}, u32[]{:S(2)}) collective-permute-start(f32[88,128]{1,0:T(8,128)} %get-tuple-element.10), channel_id=1, source_target_pairs={{0,1},{1,0},{2,3},{3,2},{4,5},{5,4},{6,7},{7,6},{8,9},{9,8},{10,11... | collective-permute-start | bytes 135176 | tf_op jit(solution)/shard_map/ppermute | solution.py:314
  6.6 6.8 %collective-permute-start = (f32[88,128]{1,0:T(8,128)}, f32[88,128]{1,0:T(8,128)S(1)}, u32[]{:S(2)}, u32[]{:S(2)}) collective-permute-start(f32[88,128]{1,0:T(8,128)} %get-tuple-element.10), channel_id=1, source_target_pairs={{1,2},{2,1},{3,4},{4,3},{5,6},{6,5},{7,8},{8,7},{9,10},{10,9},{11,... | collective-permute-start | bytes 135176 | tf_op jit(solution)/shard_map/ppermute | solution.py:314
  13.4 0.0 collective-permute-done.1.p1
  13.5 3.5 %collective-permute-start.3 = (f32[88,128]{1,0:T(8,128)S(1)}, f32[88,128]{1,0:T(8,128)S(1)}, u32[]{:S(2)}, u32[]{:S(2)}) collective-permute-start(f32[88,128]{1,0:T(8,128)S(1)} %collective-permute-done.1.p1), channel_id=1, source_target_pairs={{1,2},{2,1},{3,4},{4,3},{5,6},{6,5},{7,8},{8,7},{9,10},{10,9},{11,... | collective-permute-start | bytes 135176 | tf_op jit(solution)/shard_map/ppermute | solution.py:314
  16.9 0.0 collective-permute-done.p0
  16.9 1.9 %collective-permute-start.2 = (f32[88,128]{1,0:T(8,128)S(1)}, f32[88,128]{1,0:T(8,128)S(1)}, u32[]{:S(2)}, u32[]{:S(2)}) collective-permute-start(f32[88,128]{1,0:T(8,128)S(1)} %collective-permute-done.p0), channel_id=1, source_target_pairs={{0,1},{1,0},{2,3},{3,2},{4,5},{5,4},{6,7},{7,6},{8,9},{9,8},{10,11... | collective-permute-start | bytes 135176 | tf_op jit(solution)/shard_map/ppermute | solution.py:314
  18.9 3.3 %collective-permute-done.3.p3 = f32[88,128]{1,0:T(8,128)S(1)} collective-permute-done((f32[88,128]{1,0:T(8,128)S(1)}, f32[88,128]{1,0:T(8,128)S(1)}, u32[]{:S(2)}, u32[]{:S(2)}) %collective-permute-start.3) | collective-permute-done | bytes 45088 | tf_op jit(solution)/shard_map/ppermute | solution.py:314
  22.2 0.0 copy-start
  22.2 1.0 %copy-done = f32[19,32,128]{2,1,0:T(8,128)S(1)} copy-done((f32[19,32,128]{2,1,0:T(8,128)S(1)}, f32[19,32,128]{2,1,0:T(8,128)}, u32[]{:S(2)}) %copy-start) | copy-done | bytes 311320
  23.1 1.8 %stream_collide.1 = (f32[19,32,128]{2,1,0:T(8,128)S(1)}, f32[88,128]{1,0:T(8,128)S(1)}, f32[16,8,128]{2,1,0:T(8,128)}) custom-call(f32[19,32,128]{2,1,0:T(8,128)S(1)} %copy-done, s32[32,128]{1,0:T(8,128)S(1)} %bitcast.5, s32[1,6]{1,0:T(1,128)S(1)} %copy-done.2, f32[88,128]{1,0:T(8,128)S(1)} %collective-permute-done.p0, ...), custom_call_target="tpu_custom_call" | custom-call | tf_op jit(solution)/shard_map/stream_collide/pallas_call | solution.py:355
  24.9 4.8 %all-to-all-start = ((f32[16,8,128]{2,1,0:T(8,128)}), f32[16,8,128]{2,1,0:T(8,128)S(1)}, u32[]{:S(2)}, u32[]{:S(2)}) async-start(f32[16,8,128]{2,1,0:T(8,128)} %get-tuple-element.13), calls=%async_computation | async-start | bytes 131072 | tf_op jit(solution)/shard_map/all_to_all | solution.py:330
  29.7 3.3 %collective-permute-start.5 = (f32[88,128]{1,0:T(8,128)S(1)}, f32[88,128]{1,0:T(8,128)S(1)}, u32[]{:S(2)}, u32[]{:S(2)}) collective-permute-start(f32[88,128]{1,0:T(8,128)S(1)} %get-tuple-element.12), channel_id=1, source_target_pairs={{0,1},{1,0},{2,3},{3,2},{4,5},{5,4},{6,7},{7,6},{8,9},{9,8},{10,11... | collective-permute-start | bytes 135176 | tf_op jit(solution)/shard_map/ppermute | solution.py:314
  33.0 7.5 %collective-permute-start.4 = (f32[88,128]{1,0:T(8,128)S(1)}, f32[88,128]{1,0:T(8,128)S(1)}, u32[]{:S(2)}, u32[]{:S(2)}) collective-permute-start(f32[88,128]{1,0:T(8,128)S(1)} %get-tuple-element.12), channel_id=1, source_target_pairs={{1,2},{2,1},{3,4},{4,3},{5,6},{6,5},{7,8},{8,7},{9,10},{10,9},{11,... | collective-permute-start | bytes 135176 | tf_op jit(solution)/shard_map/ppermute | solution.py:314
  40.5 0.6 broadcast_in_dim.2
  41.1 15.5 %all-to-all-start.1 = ((f32[32,1,128]{2,1,0:T(1,128)}), f32[32,1,128]{2,1,0:T(1,128)S(1)}, u32[]{:S(2)}, u32[]{:S(2)}) async-start(f32[32,1,128]{2,1,0:T(1,128)} %broadcast_in_dim.2), calls=%async_computation.1 | async-start | bytes 32768 | tf_op jit(solution)/shard_map/all_to_all | solution.py:330
  56.6 3.3 %collective-permute-start.6 = (f32[88,128]{1,0:T(8,128)S(1)}, f32[88,128]{1,0:T(8,128)S(1)}, u32[]{:S(2)}, u32[]{:S(2)}) collective-permute-start(f32[88,128]{1,0:T(8,128)S(1)} %collective-permute-done.5.p1), channel_id=1, source_target_pairs={{1,2},{2,1},{3,4},{4,3},{5,6},{6,5},{7,8},{8,7},{9,10},{10,9},{11,... | collective-permute-start | bytes 135176 | tf_op jit(solution)/shard_map/ppermute | solution.py:314
  59.9 1.9 %collective-permute-start.7 = (f32[88,128]{1,0:T(8,128)S(1)}, f32[88,128]{1,0:T(8,128)S(1)}, u32[]{:S(2)}, u32[]{:S(2)}) collective-permute-start(f32[88,128]{1,0:T(8,128)S(1)} %collective-permute-done.4.p0), channel_id=1, source_target_pairs={{0,1},{1,0},{2,3},{3,2},{4,5},{5,4},{6,7},{7,6},{8,9},{9,8},{10,11... | collective-permute-start | bytes 135176 | tf_op jit(solution)/shard_map/ppermute | solution.py:314
  61.8 3.8 %collective-permute-done.6.p3 = f32[88,128]{1,0:T(8,128)S(1)} collective-permute-done((f32[88,128]{1,0:T(8,128)S(1)}, f32[88,128]{1,0:T(8,128)S(1)}, u32[]{:S(2)}, u32[]{:S(2)}) %collective-permute-start.6) | collective-permute-done | bytes 45088 | tf_op jit(solution)/shard_map/ppermute | solution.py:314
  65.6 0.6 pick_tiles.1.base_ref
  66.2 1.6 %stream_last.1 = f32[19,32,128]{2,1,0:T(8,128)} custom-call(f32[19,32,128]{2,1,0:T(8,128)S(1)} %get-tuple-element.11.own_ref, s32[32,128]{1,0:T(8,128)S(1)} %bitcast.6, s32[1,6]{1,0:T(1,128)S(1)} %copy-done.2, f32[88,128]{1,0:T(8,128)S(1)} %pick_tiles.1.base_ref, f32[88,128]{1,0:T(8,128)S(1)} %collective-permute-done.7.p2), custom_call_target="tpu_custom_call" | custom-call | flops 4000000 | bytes 1000000 | tf_op jit(solution)/shard_map/stream_last/pallas_call | solution.py:379
  67.7 0.6 all-to-all-done.1
  68.4 0.5 slice_multiply_fusion
  (10 shorter events, 0.1 us)
Async XLA Ops:
  0.6 21.5 %copy-start.1 = (s32[1,4096]{1,0:T(1,128)S(1)}, s32[1,4096]{1,0:T(1,128)}, u32[]{:S(2)}) copy-start(s32[1,4096]{1,0:T(1,128)} %param.4) | copy-start | bytes 49156
  2.5 19.6 %copy-start.2 = (s32[1,6]{1,0:T(1,128)S(1)}, s32[1,6]{1,0:T(1,128)}, u32[]{:S(2)}) copy-start(s32[1,6]{1,0:T(1,128)} %nb_ref.5) | copy-start | bytes 76
  2.6 10.9 %collective-permute-start.1 = (f32[88,128]{1,0:T(8,128)}, f32[88,128]{1,0:T(8,128)S(1)}, u32[]{:S(2)}, u32[]{:S(2)}) collective-permute-start(f32[88,128]{1,0:T(8,128)} %get-tuple-element.10), channel_id=1, source_target_pairs={{0,1},{1,0},{2,3},{3,2},{4,5},{5,4},{6,7},{7,6},{8,9},{9,8},{10,11... | collective-permute-start | bytes 135176 | tf_op jit(solution)/shard_map/ppermute | solution.py:314
  6.6 10.3 %collective-permute-start = (f32[88,128]{1,0:T(8,128)}, f32[88,128]{1,0:T(8,128)S(1)}, u32[]{:S(2)}, u32[]{:S(2)}) collective-permute-start(f32[88,128]{1,0:T(8,128)} %get-tuple-element.10), channel_id=1, source_target_pairs={{1,2},{2,1},{3,4},{4,3},{5,6},{6,5},{7,8},{8,7},{9,10},{10,9},{11,... | collective-permute-start | bytes 135176 | tf_op jit(solution)/shard_map/ppermute | solution.py:314
  13.5 8.7 %collective-permute-start.3 = (f32[88,128]{1,0:T(8,128)S(1)}, f32[88,128]{1,0:T(8,128)S(1)}, u32[]{:S(2)}, u32[]{:S(2)}) collective-permute-start(f32[88,128]{1,0:T(8,128)S(1)} %collective-permute-done.1.p1), channel_id=1, source_target_pairs={{1,2},{2,1},{3,4},{4,3},{5,6},{6,5},{7,8},{8,7},{9,10},{10,9},{11,... | collective-permute-start | bytes 135176 | tf_op jit(solution)/shard_map/ppermute | solution.py:314
  16.9 5.2 %collective-permute-start.2 = (f32[88,128]{1,0:T(8,128)S(1)}, f32[88,128]{1,0:T(8,128)S(1)}, u32[]{:S(2)}, u32[]{:S(2)}) collective-permute-start(f32[88,128]{1,0:T(8,128)S(1)} %collective-permute-done.p0), channel_id=1, source_target_pairs={{0,1},{1,0},{2,3},{3,2},{4,5},{5,4},{6,7},{7,6},{8,9},{9,8},{10,11... | collective-permute-start | bytes 135176 | tf_op jit(solution)/shard_map/ppermute | solution.py:314
  22.2 1.0 %copy-start = (f32[19,32,128]{2,1,0:T(8,128)S(1)}, f32[19,32,128]{2,1,0:T(8,128)}, u32[]{:S(2)}) copy-start(f32[19,32,128]{2,1,0:T(8,128)} %get-tuple-element.9.own_ref) | copy-start | bytes 933892
  24.9 15.6 %all-to-all-start = ((f32[16,8,128]{2,1,0:T(8,128)}), f32[16,8,128]{2,1,0:T(8,128)S(1)}, u32[]{:S(2)}, u32[]{:S(2)}) async-start(f32[16,8,128]{2,1,0:T(8,128)} %get-tuple-element.13), calls=%async_computation | async-start | bytes 131072 | tf_op jit(solution)/shard_map/all_to_all | solution.py:330
  29.7 10.8 %collective-permute-start.5 = (f32[88,128]{1,0:T(8,128)S(1)}, f32[88,128]{1,0:T(8,128)S(1)}, u32[]{:S(2)}, u32[]{:S(2)}) collective-permute-start(f32[88,128]{1,0:T(8,128)S(1)} %get-tuple-element.12), channel_id=1, source_target_pairs={{0,1},{1,0},{2,3},{3,2},{4,5},{5,4},{6,7},{7,6},{8,9},{9,8},{10,11... | collective-permute-start | bytes 135176 | tf_op jit(solution)/shard_map/ppermute | solution.py:314
  33.0 26.9 %collective-permute-start.4 = (f32[88,128]{1,0:T(8,128)S(1)}, f32[88,128]{1,0:T(8,128)S(1)}, u32[]{:S(2)}, u32[]{:S(2)}) collective-permute-start(f32[88,128]{1,0:T(8,128)S(1)} %get-tuple-element.12), channel_id=1, source_target_pairs={{1,2},{2,1},{3,4},{4,3},{5,6},{6,5},{7,8},{8,7},{9,10},{10,9},{11,... | collective-permute-start | bytes 135176 | tf_op jit(solution)/shard_map/ppermute | solution.py:314
  41.1 27.2 %all-to-all-start.1 = ((f32[32,1,128]{2,1,0:T(1,128)}), f32[32,1,128]{2,1,0:T(1,128)S(1)}, u32[]{:S(2)}, u32[]{:S(2)}) async-start(f32[32,1,128]{2,1,0:T(1,128)} %broadcast_in_dim.2), calls=%async_computation.1 | async-start | bytes 32768 | tf_op jit(solution)/shard_map/all_to_all | solution.py:330
  56.6 9.0 %collective-permute-start.6 = (f32[88,128]{1,0:T(8,128)S(1)}, f32[88,128]{1,0:T(8,128)S(1)}, u32[]{:S(2)}, u32[]{:S(2)}) collective-permute-start(f32[88,128]{1,0:T(8,128)S(1)} %collective-permute-done.5.p1), channel_id=1, source_target_pairs={{1,2},{2,1},{3,4},{4,3},{5,6},{6,5},{7,8},{8,7},{9,10},{10,9},{11,... | collective-permute-start | bytes 135176 | tf_op jit(solution)/shard_map/ppermute | solution.py:314
  59.9 6.3 %collective-permute-start.7 = (f32[88,128]{1,0:T(8,128)S(1)}, f32[88,128]{1,0:T(8,128)S(1)}, u32[]{:S(2)}, u32[]{:S(2)}) collective-permute-start(f32[88,128]{1,0:T(8,128)S(1)} %collective-permute-done.4.p0), channel_id=1, source_target_pairs={{0,1},{1,0},{2,3},{3,2},{4,5},{5,4},{6,7},{7,6},{8,9},{9,8},{10,11... | collective-permute-start | bytes 135176 | tf_op jit(solution)/shard_map/ppermute | solution.py:314

commit v4 on v3

--- a/solution.py
+++ b/solution.py
@@ -228,13 +228,7 @@
         put(i, jnp.where(wet, value, 0.0), open_link)
 
 
-def first_kernel(pop_hbm, fluid_hbm, post_ref, pack_ref, pop_ref, fluid_ref, sems):
-    pop_copy = pltpu.make_async_copy(pop_hbm, pop_ref, sems.at[0])
-    fluid_copy = pltpu.make_async_copy(fluid_hbm, fluid_ref, sems.at[1])
-    pop_copy.start()
-    fluid_copy.start()
-    fluid_copy.wait()
-    pop_copy.wait()
+def first_kernel(pop_ref, fluid_ref, post_ref, pack_ref):
     grid = Grid()
     wet = fluid_ref[...] > 0
     g = collide([pop_ref[i] for i in range(19)], wet)
@@ -345,10 +339,9 @@
     post, pack = pl.pallas_call(
         first_kernel,
         out_shape=(cube, packed),
-        in_specs=[pl.BlockSpec(memory_space=pltpu.HBM)] * 2,
+        in_specs=vmem(2),
         out_specs=tuple(vmem(2)),
-        scratch_shapes=[scratch, pltpu.VMEM((ROWS, LANES), jnp.int32), pltpu.SemaphoreType.DMA((2,))],
-        compiler_params=pltpu.CompilerParams(vmem_limit_bytes=60 * 2**20),
+        compiler_params=params,
         name="collide_first",
     )(pop, wall)
     ghosts = pass_on(*exchange(pack))

time: 69.4 us -> 68.7 us (0.990)
  Pallas kernels: 5.79 us -> 4.18 us
  local copies, waits for them, and re-layouts: 1.59 us -> 2.3 us
    pallas_call x1, Pallas kernels: 1.89 us -> 0.28 us  [shards(): pl.pallas_call(first_kernel, out_shape=(cube, packed), in_specs=vmem(2),...]
    unnamed x6 -> x8, local copies, waits for them, and re-layouts: 0.97 us -> 1.69 us
where the time goes in v4:
time: 68.7 us; the launch traced here: 68.1 us
  starting transfers between devices  52.4 us (76%)
  waiting for transfers between devices  7.9 us (11%)
  Pallas kernels  4.18 us (6%)
  local copies, waits for them, and re-layouts  2.3 us (3%)
  between operations  0.81 us (1%)
    ppermute x8, starting transfers between devices, swap(): return lax.ppermute(pack, ('node', 'local'), pairs)  32.1 us
    all_to_all x2, starting transfers between devices, spread_out(): return lax.all_to_all(lines, axis, 0, 0, tiled=True)  20.3 us
    ppermute x8, waiting for transfers between devices, swap(): return lax.ppermute(pack, ('node', 'local'), pairs)  7.27 us
    pallas_call x1, Pallas kernels, shards(): pl.pallas_call(middle_kernel, out_shape=(cube, packed, lines), in_specs=v...  1.76 us
    unnamed x8, local copies, waits for them, and re-layouts  1.69 us
    pallas_call x1, Pallas kernels, shards(): pl.pallas_call(last_kernel, out_shape=cube, in_specs=vmem(2) + smem + vme...  1.56 us
  transfers between devices with their start and end apart: 10, of which 3 were waited for; matrix products, arithmetic and copies ran while one was open for 1% of the time, Pallas kernels for 3%

profile of v4, /device:TPU:1, one launch (start us, length us, event | category | flops | bytes accessed | tf_op | source)
XLA Modules:
  0.0 68.1 jit_solution(5150813244042965234)
XLA Ops:
  0.6 1.0 %copy-done = f32[1,19,4096]{2,0,1:T(1,128)S(1)} copy-done((f32[1,19,4096]{2,0,1:T(1,128)S(1)}, f32[1,19,4096]{2,0,1:T(1,128)}, u32[]{:S(2)}) %copy-start) | copy-done | bytes 311320
  1.6 0.7 %copy-done.1 = s32[1,4096]{1,0:T(1,128)S(1)} copy-done((s32[1,4096]{1,0:T(1,128)S(1)}, s32[1,4096]{1,0:T(1,128)}, u32[]{:S(2)}) %copy-start.1) | copy-done | bytes 16408
  2.3 0.3 collide_first.1
  2.6 4.2 %collective-permute-start.1 = (f32[88,128]{1,0:T(8,128)S(1)}, f32[88,128]{1,0:T(8,128)S(1)}, u32[]{:S(2)}, u32[]{:S(2)}) collective-permute-start(f32[88,128]{1,0:T(8,128)S(1)} %get-tuple-element.10), channel_id=1, source_target_pairs={{0,1},{1,0},{2,3},{3,2},{4,5},{5,4},{6,7},{7,6},{8,9},{9,8},{10,11... | collective-permute-start | bytes 135176 | tf_op jit(solution)/shard_map/ppermute | solution.py:308
  6.8 6.8 %collective-permute-start = (f32[88,128]{1,0:T(8,128)S(1)}, f32[88,128]{1,0:T(8,128)S(1)}, u32[]{:S(2)}, u32[]{:S(2)}) collective-permute-start(f32[88,128]{1,0:T(8,128)S(1)} %get-tuple-element.10), channel_id=1, source_target_pairs={{1,2},{2,1},{3,4},{4,3},{5,6},{6,5},{7,8},{8,7},{9,10},{10,9},{11,... | collective-permute-start | bytes 135176 | tf_op jit(solution)/shard_map/ppermute | solution.py:308
  13.6 0.0 collective-permute-done.1.p1
  13.6 3.3 %collective-permute-start.3 = (f32[88,128]{1,0:T(8,128)S(1)}, f32[88,128]{1,0:T(8,128)S(1)}, u32[]{:S(2)}, u32[]{:S(2)}) collective-permute-start(f32[88,128]{1,0:T(8,128)S(1)} %collective-permute-done.1.p1), channel_id=1, source_target_pairs={{1,2},{2,1},{3,4},{4,3},{5,6},{6,5},{7,8},{8,7},{9,10},{10,9},{11,... | collective-permute-start | bytes 135176 | tf_op jit(solution)/shard_map/ppermute | solution.py:308
  16.9 1.9 %collective-permute-start.2 = (f32[88,128]{1,0:T(8,128)S(1)}, f32[88,128]{1,0:T(8,128)S(1)}, u32[]{:S(2)}, u32[]{:S(2)}) collective-permute-start(f32[88,128]{1,0:T(8,128)S(1)} %collective-permute-done.p0), channel_id=1, source_target_pairs={{0,1},{1,0},{2,3},{3,2},{4,5},{5,4},{6,7},{7,6},{8,9},{9,8},{10,11... | collective-permute-start | bytes 135176 | tf_op jit(solution)/shard_map/ppermute | solution.py:308
  18.8 3.5 %collective-permute-done.3.p3 = f32[88,128]{1,0:T(8,128)S(1)} collective-permute-done((f32[88,128]{1,0:T(8,128)S(1)}, f32[88,128]{1,0:T(8,128)S(1)}, u32[]{:S(2)}, u32[]{:S(2)}) %collective-permute-start.3) | collective-permute-done | bytes 45088 | tf_op jit(solution)/shard_map/ppermute | solution.py:308
  22.3 0.0 collective-permute-done.2.p2
  22.3 1.8 %stream_collide.1 = (f32[19,32,128]{2,1,0:T(8,128)S(1)}, f32[88,128]{1,0:T(8,128)S(1)}, f32[16,8,128]{2,1,0:T(8,128)}) custom-call(f32[19,32,128]{2,1,0:T(8,128)S(1)} %get-tuple-element.9.own_ref, s32[32,128]{1,0:T(8,128)S(1)} %bitcast.6, s32[1,6]{1,0:T(1,128)S(1)} %copy-done.3, f32[88,128]{1,0:T(8,128)S(1)} %collective-permute-done.p0, ...), custom_call_target="tpu_custom_call" | custom-call | tf_op jit(solution)/shard_map/stream_collide/pallas_call | solution.py:348
  24.1 4.8 %all-to-all-start = ((f32[16,8,128]{2,1,0:T(8,128)}), f32[16,8,128]{2,1,0:T(8,128)S(1)}, u32[]{:S(2)}, u32[]{:S(2)}) async-start(f32[16,8,128]{2,1,0:T(8,128)} %get-tuple-element.13), calls=%async_computation | async-start | bytes 131072 | tf_op jit(solution)/shard_map/all_to_all | solution.py:324
  28.9 3.3 %collective-permute-start.5 = (f32[88,128]{1,0:T(8,128)S(1)}, f32[88,128]{1,0:T(8,128)S(1)}, u32[]{:S(2)}, u32[]{:S(2)}) collective-permute-start(f32[88,128]{1,0:T(8,128)S(1)} %get-tuple-element.12), channel_id=1, source_target_pairs={{0,1},{1,0},{2,3},{3,2},{4,5},{5,4},{6,7},{7,6},{8,9},{9,8},{10,11... | collective-permute-start | bytes 135176 | tf_op jit(solution)/shard_map/ppermute | solution.py:308
  32.2 7.5 %collective-permute-start.4 = (f32[88,128]{1,0:T(8,128)S(1)}, f32[88,128]{1,0:T(8,128)S(1)}, u32[]{:S(2)}, u32[]{:S(2)}) collective-permute-start(f32[88,128]{1,0:T(8,128)S(1)} %get-tuple-element.12), channel_id=1, source_target_pairs={{1,2},{2,1},{3,4},{4,3},{5,6},{6,5},{7,8},{8,7},{9,10},{10,9},{11,... | collective-permute-start | bytes 135176 | tf_op jit(solution)/shard_map/ppermute | solution.py:308
  39.7 0.6 broadcast_in_dim.2
  40.3 15.5 %all-to-all-start.1 = ((f32[32,1,128]{2,1,0:T(1,128)}), f32[32,1,128]{2,1,0:T(1,128)S(1)}, u32[]{:S(2)}, u32[]{:S(2)}) async-start(f32[32,1,128]{2,1,0:T(1,128)} %broadcast_in_dim.2), calls=%async_computation.1 | async-start | bytes 32768 | tf_op jit(solution)/shard_map/all_to_all | solution.py:324
  55.8 0.0 copy-start.2
  55.8 3.3 %collective-permute-start.6 = (f32[88,128]{1,0:T(8,128)S(1)}, f32[88,128]{1,0:T(8,128)S(1)}, u32[]{:S(2)}, u32[]{:S(2)}) collective-permute-start(f32[88,128]{1,0:T(8,128)S(1)} %collective-permute-done.5.p1), channel_id=1, source_target_pairs={{1,2},{2,1},{3,4},{4,3},{5,6},{6,5},{7,8},{8,7},{9,10},{10,9},{11,... | collective-permute-start | bytes 135176 | tf_op jit(solution)/shard_map/ppermute | solution.py:308
  59.1 1.9 %collective-permute-start.7 = (f32[88,128]{1,0:T(8,128)S(1)}, f32[88,128]{1,0:T(8,128)S(1)}, u32[]{:S(2)}, u32[]{:S(2)}) collective-permute-start(f32[88,128]{1,0:T(8,128)S(1)} %collective-permute-done.4.p0), channel_id=1, source_target_pairs={{0,1},{1,0},{2,3},{3,2},{4,5},{5,4},{6,7},{7,6},{8,9},{9,8},{10,11... | collective-permute-start | bytes 135176 | tf_op jit(solution)/shard_map/ppermute | solution.py:308
  61.0 3.8 %collective-permute-done.6.p3 = f32[88,128]{1,0:T(8,128)S(1)} collective-permute-done((f32[88,128]{1,0:T(8,128)S(1)}, f32[88,128]{1,0:T(8,128)S(1)}, u32[]{:S(2)}, u32[]{:S(2)}) %collective-permute-start.6) | collective-permute-done | bytes 45088 | tf_op jit(solution)/shard_map/ppermute | solution.py:308
  64.8 0.6 pick_tiles.1.base_ref
  65.4 1.6 %stream_last.1 = f32[19,32,128]{2,1,0:T(8,128)} custom-call(f32[19,32,128]{2,1,0:T(8,128)S(1)} %get-tuple-element.11.own_ref, s32[32,128]{1,0:T(8,128)S(1)} %bitcast.7, s32[1,6]{1,0:T(1,128)S(1)} %copy-done.3, f32[88,128]{1,0:T(8,128)S(1)} %pick_tiles.1.base_ref, f32[88,128]{1,0:T(8,128)S(1)} %collective-permute-done.7.p2), custom_call_target="tpu_custom_call" | custom-call | flops 4000000 | bytes 1000000 | tf_op jit(solution)/shard_map/stream_last/pallas_call | solution.py:372
  67.0 0.6 all-to-all-done.1
  67.6 0.5 slice_multiply_fusion
  (12 shorter events, 0.1 us)
Async XLA Ops:
  0.6 1.0 %copy-start = (f32[1,19,4096]{2,0,1:T(1,128)S(1)}, f32[1,19,4096]{2,0,1:T(1,128)}, u32[]{:S(2)}) copy-start(f32[1,19,4096]{2,0,1:T(1,128)} %param.3) | copy-start | bytes 933892
  1.6 0.7 %copy-start.1 = (s32[1,4096]{1,0:T(1,128)S(1)}, s32[1,4096]{1,0:T(1,128)}, u32[]{:S(2)}) copy-start(s32[1,4096]{1,0:T(1,128)} %param.4) | copy-start | bytes 49156
  2.6 19.7 %copy-start.3 = (s32[1,6]{1,0:T(1,128)S(1)}, s32[1,6]{1,0:T(1,128)}, u32[]{:S(2)}) copy-start(s32[1,6]{1,0:T(1,128)} %nb_ref.5) | copy-start | bytes 76
  2.6 11.0 %collective-permute-start.1 = (f32[88,128]{1,0:T(8,128)S(1)}, f32[88,128]{1,0:T(8,128)S(1)}, u32[]{:S(2)}, u32[]{:S(2)}) collective-permute-start(f32[88,128]{1,0:T(8,128)S(1)} %get-tuple-element.10), channel_id=1, source_target_pairs={{0,1},{1,0},{2,3},{3,2},{4,5},{5,4},{6,7},{7,6},{8,9},{9,8},{10,11... | collective-permute-start | bytes 135176 | tf_op jit(solution)/shard_map/ppermute | solution.py:308
  6.8 10.1 %collective-permute-start = (f32[88,128]{1,0:T(8,128)S(1)}, f32[88,128]{1,0:T(8,128)S(1)}, u32[]{:S(2)}, u32[]{:S(2)}) collective-permute-start(f32[88,128]{1,0:T(8,128)S(1)} %get-tuple-element.10), channel_id=1, source_target_pairs={{1,2},{2,1},{3,4},{4,3},{5,6},{6,5},{7,8},{8,7},{9,10},{10,9},{11,... | collective-permute-start | bytes 135176 | tf_op jit(solution)/shard_map/ppermute | solution.py:308
  13.6 8.7 %collective-permute-start.3 = (f32[88,128]{1,0:T(8,128)S(1)}, f32[88,128]{1,0:T(8,128)S(1)}, u32[]{:S(2)}, u32[]{:S(2)}) collective-permute-start(f32[88,128]{1,0:T(8,128)S(1)} %collective-permute-done.1.p1), channel_id=1, source_target_pairs={{1,2},{2,1},{3,4},{4,3},{5,6},{6,5},{7,8},{8,7},{9,10},{10,9},{11,... | collective-permute-start | bytes 135176 | tf_op jit(solution)/shard_map/ppermute | solution.py:308
  16.9 5.4 %collective-permute-start.2 = (f32[88,128]{1,0:T(8,128)S(1)}, f32[88,128]{1,0:T(8,128)S(1)}, u32[]{:S(2)}, u32[]{:S(2)}) collective-permute-start(f32[88,128]{1,0:T(8,128)S(1)} %collective-permute-done.p0), channel_id=1, source_target_pairs={{0,1},{1,0},{2,3},{3,2},{4,5},{5,4},{6,7},{7,6},{8,9},{9,8},{10,11... | collective-permute-start | bytes 135176 | tf_op jit(solution)/shard_map/ppermute | solution.py:308
  24.1 15.6 %all-to-all-start = ((f32[16,8,128]{2,1,0:T(8,128)}), f32[16,8,128]{2,1,0:T(8,128)S(1)}, u32[]{:S(2)}, u32[]{:S(2)}) async-start(f32[16,8,128]{2,1,0:T(8,128)} %get-tuple-element.13), calls=%async_computation | async-start | bytes 131072 | tf_op jit(solution)/shard_map/all_to_all | solution.py:324
  28.9 10.8 %collective-permute-start.5 = (f32[88,128]{1,0:T(8,128)S(1)}, f32[88,128]{1,0:T(8,128)S(1)}, u32[]{:S(2)}, u32[]{:S(2)}) collective-permute-start(f32[88,128]{1,0:T(8,128)S(1)} %get-tuple-element.12), channel_id=1, source_target_pairs={{0,1},{1,0},{2,3},{3,2},{4,5},{5,4},{6,7},{7,6},{8,9},{9,8},{10,11... | collective-permute-start | bytes 135176 | tf_op jit(solution)/shard_map/ppermute | solution.py:308
  32.2 26.9 %collective-permute-start.4 = (f32[88,128]{1,0:T(8,128)S(1)}, f32[88,128]{1,0:T(8,128)S(1)}, u32[]{:S(2)}, u32[]{:S(2)}) collective-permute-start(f32[88,128]{1,0:T(8,128)S(1)} %get-tuple-element.12), channel_id=1, source_target_pairs={{1,2},{2,1},{3,4},{4,3},{5,6},{6,5},{7,8},{8,7},{9,10},{10,9},{11,... | collective-permute-start | bytes 135176 | tf_op jit(solution)/shard_map/ppermute | solution.py:308
  40.3 27.2 %all-to-all-start.1 = ((f32[32,1,128]{2,1,0:T(1,128)}), f32[32,1,128]{2,1,0:T(1,128)S(1)}, u32[]{:S(2)}, u32[]{:S(2)}) async-start(f32[32,1,128]{2,1,0:T(1,128)} %broadcast_in_dim.2), calls=%async_computation.1 | async-start | bytes 32768 | tf_op jit(solution)/shard_map/all_to_all | solution.py:324
  55.8 9.6 %copy-start.2 = (s32[1,4096]{1,0:T(1,128)S(1)}, s32[1,4096]{1,0:T(1,128)}, u32[]{:S(2)}) copy-start(s32[1,4096]{1,0:T(1,128)} %param.4) | copy-start | bytes 49156
  55.8 9.0 %collective-permute-start.6 = (f32[88,128]{1,0:T(8,128)S(1)}, f32[88,128]{1,0:T(8,128)S(1)}, u32[]{:S(2)}, u32[]{:S(2)}) collective-permute-start(f32[88,128]{1,0:T(8,128)S(1)} %collective-permute-done.5.p1), channel_id=1, source_target_pairs={{1,2},{2,1},{3,4},{4,3},{5,6},{6,5},{7,8},{8,7},{9,10},{10,9},{11,... | collective-permute-start | bytes 135176 | tf_op jit(solution)/shard_map/ppermute | solution.py:308
  59.1 6.3 %collective-permute-start.7 = (f32[88,128]{1,0:T(8,128)S(1)}, f32[88,128]{1,0:T(8,128)S(1)}, u32[]{:S(2)}, u32[]{:S(2)}) collective-permute-start(f32[88,128]{1,0:T(8,128)S(1)} %collective-permute-done.4.p0), channel_id=1, source_target_pairs={{0,1},{1,0},{2,3},{3,2},{4,5},{5,4},{6,7},{7,6},{8,9},{9,8},{10,11... | collective-permute-start | bytes 135176 | tf_op jit(solution)/shard_map/ppermute | solution.py:308

commit v5 on v4

--- a/solution.py
+++ b/solution.py
@@ -320,15 +320,22 @@
     return [other, mate, past_mate, past_other]
 
 
-def spread_out(lines, axis):
-    return lax.all_to_all(lines, axis, 0, 0, tiled=True)
+CORES = 2
+
+
+def spread_out(lines, groups):
+    return lax.all_to_all(lines, ("node", "local"), 0, 0, tiled=True, axis_index_groups=groups)
 
 
 def shards(populations, fluid, neighbours):
     f32 = jnp.float32
     cube = jax.ShapeDtypeStruct((19, ROWS, LANES), f32)
     packed = jax.ShapeDtypeStruct((PACK_ROWS, LANES), f32)
-    lines = jax.ShapeDtypeStruct((lax.axis_size("local"), 8, LANES), f32)
+    layer = CORES * lax.axis_size("local")
+    layers = lax.axis_size("node") // CORES
+    in_layer = [[z * layer + i for i in range(layer)] for z in range(layers)]
+    across_layers = [[z * layer + i for z in range(layers)] for i in range(layer)]
+    lines = jax.ShapeDtypeStruct((layer, 4, LANES), f32)
     scratch = pltpu.VMEM((19, ROWS, LANES), f32)
     smem = [pl.BlockSpec(memory_space=pltpu.SMEM)]
     devices = lax.axis_size("node") * lax.axis_size("local")
@@ -354,11 +361,11 @@
         compiler_params=params,
         name="stream_collide",
     )(post, wall, neighbours, *ghosts)
-    sums = spread_out(sums, "local")
+    sums = spread_out(sums, in_layer)
     other, mate = exchange(pack)
     sums, mate = lax.optimization_barrier((sums, mate))
-    plane = jnp.sum(sums[:, 0, :], axis=0, keepdims=True)
-    sums = spread_out(jnp.broadcast_to(plane, (lax.axis_size("node"), LANES)), "node")
+    plane = jnp.sum(sums[:, 0, :], axis=0)[None, None]
+    sums = spread_out(jnp.broadcast_to(plane, (layers, 4, LANES)), across_layers)
     other, mate, past_mate, past_other = pass_on(other, mate)
     tile = pl.pallas_call(
         pick_kernel,
@@ -379,7 +386,7 @@
         name="stream_last",
         cost_estimate=pl.CostEstimate(flops=4000000, bytes_accessed=1000000, transcendentals=0),
     )(post, wall, neighbours, tile, past_mate)
-    flow = jnp.sum(sums, axis=0)[:3] / (devices * BLK * BLK)
+    flow = jnp.sum(sums[:, 0, :3], axis=0) / (devices * BLK * BLK)
     return out.reshape(populations.shape), flow
 
 

time: 68.7 us -> 70.9 us (1.032)
  waiting for transfers between devices: 7.9 us -> 11.2 us
  starting transfers between devices: 52.4 us -> 51.3 us
    ppermute x8, waiting for transfers between devices: 7.27 us -> 9.2 us  [swap(): return lax.ppermute(pack, ('node', 'local'), pairs)]
    ppermute x8, starting transfers between devices: 32.1 us -> 30.3 us  [swap(): return lax.ppermute(pack, ('node', 'local'), pairs)]
    all_to_all x2, waiting for transfers between devices: 0.62 us -> 1.97 us  [spread_out(): lax.all_to_all(lines, ('node', 'local'), 0, 0, tiled=True, axis_index_gro...]
    all_to_all x2, starting transfers between devices: 20.3 us -> 21 us  [spread_out(): lax.all_to_all(lines, ('node', 'local'), 0, 0, tiled=True, axis_index_gro...]
  transfers between devices with their start and end apart: 10 -> 10, of which waited for: 3 -> 5; matrix products, arithmetic and copies ran while one was open for 1% -> 0% of each run, Pallas kernels for 3% -> 3%
where the time goes in v5:
time: 70.9 us; the launch traced here: 70.3 us
  starting transfers between devices  51.3 us (72%)
  waiting for transfers between devices  11.2 us (16%)
  Pallas kernels  4.19 us (6%)
  local copies, waits for them, and re-layouts  2.31 us (3%)
  between operations  0.79 us (1%)
    ppermute x8, starting transfers between devices, swap(): return lax.ppermute(pack, ('node', 'local'), pairs)  30.3 us
    all_to_all x2, starting transfers between devices, spread_out(): lax.all_to_all(lines, ('node', 'local'), 0, 0, tiled=True, axis_index_gro...  21 us
    ppermute x8, waiting for transfers between devices, swap(): return lax.ppermute(pack, ('node', 'local'), pairs)  9.2 us
    all_to_all x2, waiting for transfers between devices, spread_out(): lax.all_to_all(lines, ('node', 'local'), 0, 0, tiled=True, axis_index_gro...  1.97 us
    pallas_call x1, Pallas kernels, shards(): pl.pallas_call(middle_kernel, out_shape=(cube, packed, lines), in_specs=v...  1.77 us
    unnamed x8, local copies, waits for them, and re-layouts  1.69 us
    pallas_call x1, Pallas kernels, shards(): pl.pallas_call(last_kernel, out_shape=cube, in_specs=vmem(2) + smem + vme...  1.56 us
  transfers between devices with their start and end apart: 10, of which 5 were waited for; matrix products, arithmetic and copies ran while one was open for 0% of the time, Pallas kernels for 3%

profile of v5, /device:TPU:1, one launch (start us, length us, event | category | flops | bytes accessed | tf_op | source)
XLA Modules:
  0.0 70.3 jit_solution(4463799071966629083)
XLA Ops:
  0.6 1.0 %copy-done = f32[1,19,4096]{2,0,1:T(1,128)S(1)} copy-done((f32[1,19,4096]{2,0,1:T(1,128)S(1)}, f32[1,19,4096]{2,0,1:T(1,128)}, u32[]{:S(2)}) %copy-start) | copy-done | bytes 311320
  1.6 0.7 %copy-done.1 = s32[1,4096]{1,0:T(1,128)S(1)} copy-done((s32[1,4096]{1,0:T(1,128)S(1)}, s32[1,4096]{1,0:T(1,128)}, u32[]{:S(2)}) %copy-start.1) | copy-done | bytes 16408
  2.3 0.3 collide_first.1
  2.6 4.2 %collective-permute-start.1 = (f32[88,128]{1,0:T(8,128)S(1)}, f32[88,128]{1,0:T(8,128)S(1)}, u32[]{:S(2)}, u32[]{:S(2)}) collective-permute-start(f32[88,128]{1,0:T(8,128)S(1)} %get-tuple-element.10), channel_id=1, source_target_pairs={{0,1},{1,0},{2,3},{3,2},{4,5},{5,4},{6,7},{7,6},{8,9},{9,8},{10,11... | collective-permute-start | bytes 135176 | tf_op jit(solution)/shard_map/ppermute | solution.py:308
  6.8 6.8 %collective-permute-start = (f32[88,128]{1,0:T(8,128)S(1)}, f32[88,128]{1,0:T(8,128)S(1)}, u32[]{:S(2)}, u32[]{:S(2)}) collective-permute-start(f32[88,128]{1,0:T(8,128)S(1)} %get-tuple-element.10), channel_id=1, source_target_pairs={{1,2},{2,1},{3,4},{4,3},{5,6},{6,5},{7,8},{8,7},{9,10},{10,9},{11,... | collective-permute-start | bytes 135176 | tf_op jit(solution)/shard_map/ppermute | solution.py:308
  13.6 3.3 %collective-permute-start.3 = (f32[88,128]{1,0:T(8,128)S(1)}, f32[88,128]{1,0:T(8,128)S(1)}, u32[]{:S(2)}, u32[]{:S(2)}) collective-permute-start(f32[88,128]{1,0:T(8,128)S(1)} %collective-permute-done.1.p1), channel_id=1, source_target_pairs={{1,2},{2,1},{3,4},{4,3},{5,6},{6,5},{7,8},{8,7},{9,10},{10,9},{11,... | collective-permute-start | bytes 135176 | tf_op jit(solution)/shard_map/ppermute | solution.py:308
  16.9 1.9 %collective-permute-start.2 = (f32[88,128]{1,0:T(8,128)S(1)}, f32[88,128]{1,0:T(8,128)S(1)}, u32[]{:S(2)}, u32[]{:S(2)}) collective-permute-start(f32[88,128]{1,0:T(8,128)S(1)} %collective-permute-done.p0), channel_id=1, source_target_pairs={{0,1},{1,0},{2,3},{3,2},{4,5},{5,4},{6,7},{7,6},{8,9},{9,8},{10,11... | collective-permute-start | bytes 135176 | tf_op jit(solution)/shard_map/ppermute | solution.py:308
  18.8 3.5 %collective-permute-done.3.p3 = f32[88,128]{1,0:T(8,128)S(1)} collective-permute-done((f32[88,128]{1,0:T(8,128)S(1)}, f32[88,128]{1,0:T(8,128)S(1)}, u32[]{:S(2)}, u32[]{:S(2)}) %collective-permute-start.3) | collective-permute-done | bytes 45088 | tf_op jit(solution)/shard_map/ppermute | solution.py:308
  22.3 1.8 %stream_collide.1 = (f32[19,32,128]{2,1,0:T(8,128)S(1)}, f32[88,128]{1,0:T(8,128)S(1)}, f32[32,4,128]{2,1,0:T(4,128)}) custom-call(f32[19,32,128]{2,1,0:T(8,128)S(1)} %get-tuple-element.9.own_ref, s32[32,128]{1,0:T(8,128)S(1)} %bitcast.5, s32[1,6]{1,0:T(1,128)S(1)} %copy-done.3, f32[88,128]{1,0:T(8,128)S(1)} %collective-permute-done.p0, ...), custom_call_target="tpu_custom_call" | custom-call | tf_op jit(solution)/shard_map/stream_collide/pallas_call | solution.py:355
  24.1 6.1 %all-to-all-start = ((f32[32,4,128]{2,1,0:T(4,128)}), f32[32,4,128]{2,1,0:T(4,128)S(1)}, u32[]{:S(2)}, u32[]{:S(2)}) async-start(f32[32,4,128]{2,1,0:T(4,128)} %get-tuple-element.13), calls=%async_computation | async-start | bytes 131072 | tf_op jit(solution)/shard_map/all_to_all | solution.py:327
  30.2 3.3 %collective-permute-start.5 = (f32[88,128]{1,0:T(8,128)S(1)}, f32[88,128]{1,0:T(8,128)S(1)}, u32[]{:S(2)}, u32[]{:S(2)}) collective-permute-start(f32[88,128]{1,0:T(8,128)S(1)} %get-tuple-element.12), channel_id=1, source_target_pairs={{0,1},{1,0},{2,3},{3,2},{4,5},{5,4},{6,7},{7,6},{8,9},{9,8},{10,11... | collective-permute-start | bytes 135176 | tf_op jit(solution)/shard_map/ppermute | solution.py:308
  33.5 1.9 %collective-permute-done.5.p1 = f32[88,128]{1,0:T(8,128)S(1)} collective-permute-done((f32[88,128]{1,0:T(8,128)S(1)}, f32[88,128]{1,0:T(8,128)S(1)}, u32[]{:S(2)}, u32[]{:S(2)}) %collective-permute-start.5) | collective-permute-done | bytes 45088 | tf_op jit(solution)/shard_map/ppermute | solution.py:308
  35.4 2.0 %all-to-all-done = f32[32,4,128]{2,1,0:T(4,128)S(1)} async-done(((f32[32,4,128]{2,1,0:T(4,128)}), f32[32,4,128]{2,1,0:T(4,128)S(1)}, u32[]{:S(2)}, u32[]{:S(2)}) %all-to-all-start) | async-done | bytes 65568 | tf_op jit(solution)/shard_map/all_to_all | solution.py:327
  37.4 0.6 broadcast_in_dim.2
  38.0 14.9 %all-to-all-start.1 = ((f32[16,4,128]{2,1,0:T(4,128)}), f32[16,4,128]{2,1,0:T(4,128)S(1)}, u32[]{:S(2)}, u32[]{:S(2)}) async-start(f32[16,4,128]{2,1,0:T(4,128)} %broadcast_in_dim.2), calls=%async_computation.1 | async-start | bytes 65536 | tf_op jit(solution)/shard_map/all_to_all | solution.py:327
  52.9 0.0 copy-start.2
  53.0 5.9 %collective-permute-start.4 = (f32[88,128]{1,0:T(8,128)S(1)}, f32[88,128]{1,0:T(8,128)S(1)}, u32[]{:S(2)}, u32[]{:S(2)}) collective-permute-start(f32[88,128]{1,0:T(8,128)S(1)} %get-tuple-element.12), channel_id=1, source_target_pairs={{1,2},{2,1},{3,4},{4,3},{5,6},{6,5},{7,8},{8,7},{9,10},{10,9},{11,... | collective-permute-start | bytes 135176 | tf_op jit(solution)/shard_map/ppermute | solution.py:308
  58.9 2.9 %collective-permute-start.6 = (f32[88,128]{1,0:T(8,128)S(1)}, f32[88,128]{1,0:T(8,128)S(1)}, u32[]{:S(2)}, u32[]{:S(2)}) collective-permute-start(f32[88,128]{1,0:T(8,128)S(1)} %collective-permute-done.5.p1), channel_id=1, source_target_pairs={{1,2},{2,1},{3,4},{4,3},{5,6},{6,5},{7,8},{8,7},{9,10},{10,9},{11,... | collective-permute-start | bytes 135176 | tf_op jit(solution)/shard_map/ppermute | solution.py:308
  61.8 0.1 collective-permute-done.4.p0
  61.9 1.9 %collective-permute-start.7 = (f32[88,128]{1,0:T(8,128)S(1)}, f32[88,128]{1,0:T(8,128)S(1)}, u32[]{:S(2)}, u32[]{:S(2)}) collective-permute-start(f32[88,128]{1,0:T(8,128)S(1)} %collective-permute-done.4.p0), channel_id=1, source_target_pairs={{0,1},{1,0},{2,3},{3,2},{4,5},{5,4},{6,7},{7,6},{8,9},{9,8},{10,11... | collective-permute-start | bytes 135176 | tf_op jit(solution)/shard_map/ppermute | solution.py:308
  63.8 3.7 %collective-permute-done.6.p3 = f32[88,128]{1,0:T(8,128)S(1)} collective-permute-done((f32[88,128]{1,0:T(8,128)S(1)}, f32[88,128]{1,0:T(8,128)S(1)}, u32[]{:S(2)}, u32[]{:S(2)}) %collective-permute-start.6) | collective-permute-done | bytes 45088 | tf_op jit(solution)/shard_map/ppermute | solution.py:308
  67.6 0.6 pick_tiles.1.base_ref
  68.2 1.6 %stream_last.1 = f32[19,32,128]{2,1,0:T(8,128)} custom-call(f32[19,32,128]{2,1,0:T(8,128)S(1)} %get-tuple-element.11.own_ref, s32[32,128]{1,0:T(8,128)S(1)} %bitcast.6, s32[1,6]{1,0:T(1,128)S(1)} %copy-done.3, f32[88,128]{1,0:T(8,128)S(1)} %pick_tiles.1.base_ref, f32[88,128]{1,0:T(8,128)S(1)} %collective-permute-done.7.p2), custom_call_target="tpu_custom_call" | custom-call | flops 4000000 | bytes 1000000 | tf_op jit(solution)/shard_map/stream_last/pallas_call | solution.py:379
  69.8 0.5 broadcast_multiply_fusion
  (12 shorter events, 0.1 us)
Async XLA Ops:
  0.6 1.0 %copy-start = (f32[1,19,4096]{2,0,1:T(1,128)S(1)}, f32[1,19,4096]{2,0,1:T(1,128)}, u32[]{:S(2)}) copy-start(f32[1,19,4096]{2,0,1:T(1,128)} %param.3) | copy-start | bytes 933892
  1.6 0.7 %copy-start.1 = (s32[1,4096]{1,0:T(1,128)S(1)}, s32[1,4096]{1,0:T(1,128)}, u32[]{:S(2)}) copy-start(s32[1,4096]{1,0:T(1,128)} %param.4) | copy-start | bytes 49156
  2.6 19.7 %copy-start.3 = (s32[1,6]{1,0:T(1,128)S(1)}, s32[1,6]{1,0:T(1,128)}, u32[]{:S(2)}) copy-start(s32[1,6]{1,0:T(1,128)} %nb_ref.5) | copy-start | bytes 76
  2.6 11.0 %collective-permute-start.1 = (f32[88,128]{1,0:T(8,128)S(1)}, f32[88,128]{1,0:T(8,128)S(1)}, u32[]{:S(2)}, u32[]{:S(2)}) collective-permute-start(f32[88,128]{1,0:T(8,128)S(1)} %get-tuple-element.10), channel_id=1, source_target_pairs={{0,1},{1,0},{2,3},{3,2},{4,5},{5,4},{6,7},{7,6},{8,9},{9,8},{10,11... | collective-permute-start | bytes 135176 | tf_op jit(solution)/shard_map/ppermute | solution.py:308
  6.8 10.1 %collective-permute-start = (f32[88,128]{1,0:T(8,128)S(1)}, f32[88,128]{1,0:T(8,128)S(1)}, u32[]{:S(2)}, u32[]{:S(2)}) collective-permute-start(f32[88,128]{1,0:T(8,128)S(1)} %get-tuple-element.10), channel_id=1, source_target_pairs={{1,2},{2,1},{3,4},{4,3},{5,6},{6,5},{7,8},{8,7},{9,10},{10,9},{11,... | collective-permute-start | bytes 135176 | tf_op jit(solution)/shard_map/ppermute | solution.py:308
  13.6 8.7 %collective-permute-start.3 = (f32[88,128]{1,0:T(8,128)S(1)}, f32[88,128]{1,0:T(8,128)S(1)}, u32[]{:S(2)}, u32[]{:S(2)}) collective-permute-start(f32[88,128]{1,0:T(8,128)S(1)} %collective-permute-done.1.p1), channel_id=1, source_target_pairs={{1,2},{2,1},{3,4},{4,3},{5,6},{6,5},{7,8},{8,7},{9,10},{10,9},{11,... | collective-permute-start | bytes 135176 | tf_op jit(solution)/shard_map/ppermute | solution.py:308
  16.9 5.4 %collective-permute-start.2 = (f32[88,128]{1,0:T(8,128)S(1)}, f32[88,128]{1,0:T(8,128)S(1)}, u32[]{:S(2)}, u32[]{:S(2)}) collective-permute-start(f32[88,128]{1,0:T(8,128)S(1)} %collective-permute-done.p0), channel_id=1, source_target_pairs={{0,1},{1,0},{2,3},{3,2},{4,5},{5,4},{6,7},{7,6},{8,9},{9,8},{10,11... | collective-permute-start | bytes 135176 | tf_op jit(solution)/shard_map/ppermute | solution.py:308
  24.1 13.2 %all-to-all-start = ((f32[32,4,128]{2,1,0:T(4,128)}), f32[32,4,128]{2,1,0:T(4,128)S(1)}, u32[]{:S(2)}, u32[]{:S(2)}) async-start(f32[32,4,128]{2,1,0:T(4,128)} %get-tuple-element.13), calls=%async_computation | async-start | bytes 131072 | tf_op jit(solution)/shard_map/all_to_all | solution.py:327
  30.2 5.2 %collective-permute-start.5 = (f32[88,128]{1,0:T(8,128)S(1)}, f32[88,128]{1,0:T(8,128)S(1)}, u32[]{:S(2)}, u32[]{:S(2)}) collective-permute-start(f32[88,128]{1,0:T(8,128)S(1)} %get-tuple-element.12), channel_id=1, source_target_pairs={{0,1},{1,0},{2,3},{3,2},{4,5},{5,4},{6,7},{7,6},{8,9},{9,8},{10,11... | collective-permute-start | bytes 135176 | tf_op jit(solution)/shard_map/ppermute | solution.py:308
  38.0 31.7 %all-to-all-start.1 = ((f32[16,4,128]{2,1,0:T(4,128)}), f32[16,4,128]{2,1,0:T(4,128)S(1)}, u32[]{:S(2)}, u32[]{:S(2)}) async-start(f32[16,4,128]{2,1,0:T(4,128)} %broadcast_in_dim.2), calls=%async_computation.1 | async-start | bytes 65536 | tf_op jit(solution)/shard_map/all_to_all | solution.py:327
  52.9 15.2 %copy-start.2 = (s32[1,4096]{1,0:T(1,128)S(1)}, s32[1,4096]{1,0:T(1,128)}, u32[]{:S(2)}) copy-start(s32[1,4096]{1,0:T(1,128)} %param.4) | copy-start | bytes 49156
  53.0 9.0 %collective-permute-start.4 = (f32[88,128]{1,0:T(8,128)S(1)}, f32[88,128]{1,0:T(8,128)S(1)}, u32[]{:S(2)}, u32[]{:S(2)}) collective-permute-start(f32[88,128]{1,0:T(8,128)S(1)} %get-tuple-element.12), channel_id=1, source_target_pairs={{1,2},{2,1},{3,4},{4,3},{5,6},{6,5},{7,8},{8,7},{9,10},{10,9},{11,... | collective-permute-start | bytes 135176 | tf_op jit(solution)/shard_map/ppermute | solution.py:308
  58.9 8.7 %collective-permute-start.6 = (f32[88,128]{1,0:T(8,128)S(1)}, f32[88,128]{1,0:T(8,128)S(1)}, u32[]{:S(2)}, u32[]{:S(2)}) collective-permute-start(f32[88,128]{1,0:T(8,128)S(1)} %collective-permute-done.5.p1), channel_id=1, source_target_pairs={{1,2},{2,1},{3,4},{4,3},{5,6},{6,5},{7,8},{8,7},{9,10},{10,9},{11,... | collective-permute-start | bytes 135176 | tf_op jit(solution)/shard_map/ppermute | solution.py:308
  61.9 6.2 %collective-permute-start.7 = (f32[88,128]{1,0:T(8,128)S(1)}, f32[88,128]{1,0:T(8,128)S(1)}, u32[]{:S(2)}, u32[]{:S(2)}) collective-permute-start(f32[88,128]{1,0:T(8,128)S(1)} %collective-permute-done.4.p0), channel_id=1, source_target_pairs={{0,1},{1,0},{2,3},{3,2},{4,5},{5,4},{6,7},{7,6},{8,9},{9,8},{10,11... | collective-permute-start | bytes 135176 | tf_op jit(solution)/shard_map/ppermute | solution.py:308

commit v6 on v5

--- a/solution.py
+++ b/solution.py
@@ -365,7 +365,7 @@
     other, mate = exchange(pack)
     sums, mate = lax.optimization_barrier((sums, mate))
     plane = jnp.sum(sums[:, 0, :], axis=0)[None, None]
-    sums = spread_out(jnp.broadcast_to(plane, (layers, 4, LANES)), across_layers)
+    sums = spread_out(jnp.broadcast_to(plane, (layers, 2, LANES)), across_layers)
     other, mate, past_mate, past_other = pass_on(other, mate)
     tile = pl.pallas_call(
         pick_kernel,

time: 70.9 us -> 67.9 us (0.958)
  waiting for transfers between devices: 11.2 us -> 7.35 us
  starting transfers between devices: 51.3 us -> 52.2 us
    ppermute x8, waiting for transfers between devices: 9.2 us -> 7.11 us  [swap(): return lax.ppermute(pack, ('node', 'local'), pairs)]
    all_to_all x2, waiting for transfers between devices: 1.97 us -> 0.23 us  [spread_out(): lax.all_to_all(lines, ('node', 'local'), 0, 0, tiled=True, axis_index_gro...]
    ppermute x8, starting transfers between devices: 30.3 us -> 31.1 us  [swap(): return lax.ppermute(pack, ('node', 'local'), pairs)]
  transfers between devices with their start and end apart: 10 -> 10, of which waited for: 5 -> 3; matrix products, arithmetic and copies ran while one was open for 0% -> 1% of each run, Pallas kernels for 3% -> 3%
where the time goes in v6:
time: 67.9 us; the launch traced here: 67.4 us
  starting transfers between devices  52.2 us (77%)
  waiting for transfers between devices  7.35 us (11%)
  Pallas kernels  4.19 us (6%)
  local copies, waits for them, and re-layouts  2.29 us (3%)
  between operations  0.81 us (1%)
    ppermute x8, starting transfers between devices, swap(): return lax.ppermute(pack, ('node', 'local'), pairs)  31.1 us
    all_to_all x2, starting transfers between devices, spread_out(): lax.all_to_all(lines, ('node', 'local'), 0, 0, tiled=True, axis_index_gro...  21 us
    ppermute x8, waiting for transfers between devices, swap(): return lax.ppermute(pack, ('node', 'local'), pairs)  7.11 us
    pallas_call x1, Pallas kernels, shards(): pl.pallas_call(middle_kernel, out_shape=(cube, packed, lines), in_specs=v...  1.77 us
    unnamed x8, local copies, waits for them, and re-layouts  1.69 us
    pallas_call x1, Pallas kernels, shards(): pl.pallas_call(last_kernel, out_shape=cube, in_specs=vmem(2) + smem + vme...  1.56 us
  transfers between devices with their start and end apart: 10, of which 3 were waited for; matrix products, arithmetic and copies ran while one was open for 1% of the time, Pallas kernels for 3%

profile of v6, /device:TPU:1, one launch (start us, length us, event | category | flops | bytes accessed | tf_op | source)
XLA Modules:
  0.0 67.4 jit_solution(7981720329251895647)
XLA Ops:
  0.6 1.0 %copy-done = f32[1,19,4096]{2,0,1:T(1,128)S(1)} copy-done((f32[1,19,4096]{2,0,1:T(1,128)S(1)}, f32[1,19,4096]{2,0,1:T(1,128)}, u32[]{:S(2)}) %copy-start) | copy-done | bytes 311320
  1.6 0.7 %copy-done.1 = s32[1,4096]{1,0:T(1,128)S(1)} copy-done((s32[1,4096]{1,0:T(1,128)S(1)}, s32[1,4096]{1,0:T(1,128)}, u32[]{:S(2)}) %copy-start.1) | copy-done | bytes 16408
  2.3 0.3 collide_first.1
  2.6 4.2 %collective-permute-start.1 = (f32[88,128]{1,0:T(8,128)S(1)}, f32[88,128]{1,0:T(8,128)S(1)}, u32[]{:S(2)}, u32[]{:S(2)}) collective-permute-start(f32[88,128]{1,0:T(8,128)S(1)} %get-tuple-element.10), channel_id=1, source_target_pairs={{0,1},{1,0},{2,3},{3,2},{4,5},{5,4},{6,7},{7,6},{8,9},{9,8},{10,11... | collective-permute-start | bytes 135176 | tf_op jit(solution)/shard_map/ppermute | solution.py:308
  6.8 6.8 %collective-permute-start = (f32[88,128]{1,0:T(8,128)S(1)}, f32[88,128]{1,0:T(8,128)S(1)}, u32[]{:S(2)}, u32[]{:S(2)}) collective-permute-start(f32[88,128]{1,0:T(8,128)S(1)} %get-tuple-element.10), channel_id=1, source_target_pairs={{1,2},{2,1},{3,4},{4,3},{5,6},{6,5},{7,8},{8,7},{9,10},{10,9},{11,... | collective-permute-start | bytes 135176 | tf_op jit(solution)/shard_map/ppermute | solution.py:308
  13.6 0.0 collective-permute-done.1.p1
  13.6 3.3 %collective-permute-start.3 = (f32[88,128]{1,0:T(8,128)S(1)}, f32[88,128]{1,0:T(8,128)S(1)}, u32[]{:S(2)}, u32[]{:S(2)}) collective-permute-start(f32[88,128]{1,0:T(8,128)S(1)} %collective-permute-done.1.p1), channel_id=1, source_target_pairs={{1,2},{2,1},{3,4},{4,3},{5,6},{6,5},{7,8},{8,7},{9,10},{10,9},{11,... | collective-permute-start | bytes 135176 | tf_op jit(solution)/shard_map/ppermute | solution.py:308
  16.9 1.9 %collective-permute-start.2 = (f32[88,128]{1,0:T(8,128)S(1)}, f32[88,128]{1,0:T(8,128)S(1)}, u32[]{:S(2)}, u32[]{:S(2)}) collective-permute-start(f32[88,128]{1,0:T(8,128)S(1)} %collective-permute-done.p0), channel_id=1, source_target_pairs={{0,1},{1,0},{2,3},{3,2},{4,5},{5,4},{6,7},{7,6},{8,9},{9,8},{10,11... | collective-permute-start | bytes 135176 | tf_op jit(solution)/shard_map/ppermute | solution.py:308
  18.8 3.5 %collective-permute-done.3.p3 = f32[88,128]{1,0:T(8,128)S(1)} collective-permute-done((f32[88,128]{1,0:T(8,128)S(1)}, f32[88,128]{1,0:T(8,128)S(1)}, u32[]{:S(2)}, u32[]{:S(2)}) %collective-permute-start.3) | collective-permute-done | bytes 45088 | tf_op jit(solution)/shard_map/ppermute | solution.py:308
  22.3 0.0 collective-permute-done.2.p2
  22.3 1.8 %stream_collide.1 = (f32[19,32,128]{2,1,0:T(8,128)S(1)}, f32[88,128]{1,0:T(8,128)S(1)}, f32[32,4,128]{2,1,0:T(4,128)}) custom-call(f32[19,32,128]{2,1,0:T(8,128)S(1)} %get-tuple-element.9.own_ref, s32[32,128]{1,0:T(8,128)S(1)} %bitcast.5, s32[1,6]{1,0:T(1,128)S(1)} %copy-done.3, f32[88,128]{1,0:T(8,128)S(1)} %collective-permute-done.p0, ...), custom_call_target="tpu_custom_call" | custom-call | tf_op jit(solution)/shard_map/stream_collide/pallas_call | solution.py:355
  24.1 6.1 %all-to-all-start = ((f32[32,4,128]{2,1,0:T(4,128)}), f32[32,4,128]{2,1,0:T(4,128)S(1)}, u32[]{:S(2)}, u32[]{:S(2)}) async-start(f32[32,4,128]{2,1,0:T(4,128)} %get-tuple-element.13), calls=%async_computation | async-start | bytes 131072 | tf_op jit(solution)/shard_map/all_to_all | solution.py:327
  30.2 3.3 %collective-permute-start.5 = (f32[88,128]{1,0:T(8,128)S(1)}, f32[88,128]{1,0:T(8,128)S(1)}, u32[]{:S(2)}, u32[]{:S(2)}) collective-permute-start(f32[88,128]{1,0:T(8,128)S(1)} %get-tuple-element.12), channel_id=1, source_target_pairs={{0,1},{1,0},{2,3},{3,2},{4,5},{5,4},{6,7},{7,6},{8,9},{9,8},{10,11... | collective-permute-start | bytes 135176 | tf_op jit(solution)/shard_map/ppermute | solution.py:308
  33.5 6.3 %collective-permute-start.4 = (f32[88,128]{1,0:T(8,128)S(1)}, f32[88,128]{1,0:T(8,128)S(1)}, u32[]{:S(2)}, u32[]{:S(2)}) collective-permute-start(f32[88,128]{1,0:T(8,128)S(1)} %get-tuple-element.12), channel_id=1, source_target_pairs={{1,2},{2,1},{3,4},{4,3},{5,6},{6,5},{7,8},{8,7},{9,10},{10,9},{11,... | collective-permute-start | bytes 135176 | tf_op jit(solution)/shard_map/ppermute | solution.py:308
  39.9 0.6 broadcast_in_dim.2
  40.5 14.9 %all-to-all-start.1 = ((f32[16,2,128]{2,1,0:T(2,128)}), f32[16,2,128]{2,1,0:T(2,128)S(1)}, u32[]{:S(2)}, u32[]{:S(2)}) async-start(f32[16,2,128]{2,1,0:T(2,128)} %broadcast_in_dim.2), calls=%async_computation.1 | async-start | bytes 32768 | tf_op jit(solution)/shard_map/all_to_all | solution.py:327
  55.4 0.0 copy-start.2
  55.5 3.4 %collective-permute-start.6 = (f32[88,128]{1,0:T(8,128)S(1)}, f32[88,128]{1,0:T(8,128)S(1)}, u32[]{:S(2)}, u32[]{:S(2)}) collective-permute-start(f32[88,128]{1,0:T(8,128)S(1)} %collective-permute-done.5.p1), channel_id=1, source_target_pairs={{1,2},{2,1},{3,4},{4,3},{5,6},{6,5},{7,8},{8,7},{9,10},{10,9},{11,... | collective-permute-start | bytes 135176 | tf_op jit(solution)/shard_map/ppermute | solution.py:308
  58.9 1.9 %collective-permute-start.7 = (f32[88,128]{1,0:T(8,128)S(1)}, f32[88,128]{1,0:T(8,128)S(1)}, u32[]{:S(2)}, u32[]{:S(2)}) collective-permute-start(f32[88,128]{1,0:T(8,128)S(1)} %collective-permute-done.4.p0), channel_id=1, source_target_pairs={{0,1},{1,0},{2,3},{3,2},{4,5},{5,4},{6,7},{7,6},{8,9},{9,8},{10,11... | collective-permute-start | bytes 135176 | tf_op jit(solution)/shard_map/ppermute | solution.py:308
  60.8 3.6 %collective-permute-done.6.p3 = f32[88,128]{1,0:T(8,128)S(1)} collective-permute-done((f32[88,128]{1,0:T(8,128)S(1)}, f32[88,128]{1,0:T(8,128)S(1)}, u32[]{:S(2)}, u32[]{:S(2)}) %collective-permute-start.6) | collective-permute-done | bytes 45088 | tf_op jit(solution)/shard_map/ppermute | solution.py:308
  64.4 0.6 pick_tiles.1.base_ref
  65.0 1.6 %stream_last.1 = f32[19,32,128]{2,1,0:T(8,128)} custom-call(f32[19,32,128]{2,1,0:T(8,128)S(1)} %get-tuple-element.11.own_ref, s32[32,128]{1,0:T(8,128)S(1)} %bitcast.6, s32[1,6]{1,0:T(1,128)S(1)} %copy-done.3, f32[88,128]{1,0:T(8,128)S(1)} %pick_tiles.1.base_ref, f32[88,128]{1,0:T(8,128)S(1)} %collective-permute-done.7.p2), custom_call_target="tpu_custom_call" | custom-call | flops 4000000 | bytes 1000000 | tf_op jit(solution)/shard_map/stream_last/pallas_call | solution.py:379
  66.6 0.2 all-to-all-done.1
  66.9 0.5 broadcast_multiply_fusion
  (12 shorter events, 0.1 us)
Async XLA Ops:
  0.6 1.0 %copy-start = (f32[1,19,4096]{2,0,1:T(1,128)S(1)}, f32[1,19,4096]{2,0,1:T(1,128)}, u32[]{:S(2)}) copy-start(f32[1,19,4096]{2,0,1:T(1,128)} %param.3) | copy-start | bytes 933892
  1.6 0.7 %copy-start.1 = (s32[1,4096]{1,0:T(1,128)S(1)}, s32[1,4096]{1,0:T(1,128)}, u32[]{:S(2)}) copy-start(s32[1,4096]{1,0:T(1,128)} %param.4) | copy-start | bytes 49156
  2.6 19.7 %copy-start.3 = (s32[1,6]{1,0:T(1,128)S(1)}, s32[1,6]{1,0:T(1,128)}, u32[]{:S(2)}) copy-start(s32[1,6]{1,0:T(1,128)} %nb_ref.5) | copy-start | bytes 76
  2.6 11.0 %collective-permute-start.1 = (f32[88,128]{1,0:T(8,128)S(1)}, f32[88,128]{1,0:T(8,128)S(1)}, u32[]{:S(2)}, u32[]{:S(2)}) collective-permute-start(f32[88,128]{1,0:T(8,128)S(1)} %get-tuple-element.10), channel_id=1, source_target_pairs={{0,1},{1,0},{2,3},{3,2},{4,5},{5,4},{6,7},{7,6},{8,9},{9,8},{10,11... | collective-permute-start | bytes 135176 | tf_op jit(solution)/shard_map/ppermute | solution.py:308
  6.8 10.1 %collective-permute-start = (f32[88,128]{1,0:T(8,128)S(1)}, f32[88,128]{1,0:T(8,128)S(1)}, u32[]{:S(2)}, u32[]{:S(2)}) collective-permute-start(f32[88,128]{1,0:T(8,128)S(1)} %get-tuple-element.10), channel_id=1, source_target_pairs={{1,2},{2,1},{3,4},{4,3},{5,6},{6,5},{7,8},{8,7},{9,10},{10,9},{11,... | collective-permute-start | bytes 135176 | tf_op jit(solution)/shard_map/ppermute | solution.py:308
  13.6 8.7 %collective-permute-start.3 = (f32[88,128]{1,0:T(8,128)S(1)}, f32[88,128]{1,0:T(8,128)S(1)}, u32[]{:S(2)}, u32[]{:S(2)}) collective-permute-start(f32[88,128]{1,0:T(8,128)S(1)} %collective-permute-done.1.p1), channel_id=1, source_target_pairs={{1,2},{2,1},{3,4},{4,3},{5,6},{6,5},{7,8},{8,7},{9,10},{10,9},{11,... | collective-permute-start | bytes 135176 | tf_op jit(solution)/shard_map/ppermute | solution.py:308
  16.9 5.4 %collective-permute-start.2 = (f32[88,128]{1,0:T(8,128)S(1)}, f32[88,128]{1,0:T(8,128)S(1)}, u32[]{:S(2)}, u32[]{:S(2)}) collective-permute-start(f32[88,128]{1,0:T(8,128)S(1)} %collective-permute-done.p0), channel_id=1, source_target_pairs={{0,1},{1,0},{2,3},{3,2},{4,5},{5,4},{6,7},{7,6},{8,9},{9,8},{10,11... | collective-permute-start | bytes 135176 | tf_op jit(solution)/shard_map/ppermute | solution.py:308
  24.1 15.7 %all-to-all-start = ((f32[32,4,128]{2,1,0:T(4,128)}), f32[32,4,128]{2,1,0:T(4,128)S(1)}, u32[]{:S(2)}, u32[]{:S(2)}) async-start(f32[32,4,128]{2,1,0:T(4,128)} %get-tuple-element.13), calls=%async_computation | async-start | bytes 131072 | tf_op jit(solution)/shard_map/all_to_all | solution.py:327
  30.2 9.6 %collective-permute-start.5 = (f32[88,128]{1,0:T(8,128)S(1)}, f32[88,128]{1,0:T(8,128)S(1)}, u32[]{:S(2)}, u32[]{:S(2)}) collective-permute-start(f32[88,128]{1,0:T(8,128)S(1)} %get-tuple-element.12), channel_id=1, source_target_pairs={{0,1},{1,0},{2,3},{3,2},{4,5},{5,4},{6,7},{7,6},{8,9},{9,8},{10,11... | collective-permute-start | bytes 135176 | tf_op jit(solution)/shard_map/ppermute | solution.py:308
  33.5 25.4 %collective-permute-start.4 = (f32[88,128]{1,0:T(8,128)S(1)}, f32[88,128]{1,0:T(8,128)S(1)}, u32[]{:S(2)}, u32[]{:S(2)}) collective-permute-start(f32[88,128]{1,0:T(8,128)S(1)} %get-tuple-element.12), channel_id=1, source_target_pairs={{1,2},{2,1},{3,4},{4,3},{5,6},{6,5},{7,8},{8,7},{9,10},{10,9},{11,... | collective-permute-start | bytes 135176 | tf_op jit(solution)/shard_map/ppermute | solution.py:308
  40.5 26.3 %all-to-all-start.1 = ((f32[16,2,128]{2,1,0:T(2,128)}), f32[16,2,128]{2,1,0:T(2,128)S(1)}, u32[]{:S(2)}, u32[]{:S(2)}) async-start(f32[16,2,128]{2,1,0:T(2,128)} %broadcast_in_dim.2), calls=%async_computation.1 | async-start | bytes 32768 | tf_op jit(solution)/shard_map/all_to_all | solution.py:327
  55.4 9.6 %copy-start.2 = (s32[1,4096]{1,0:T(1,128)S(1)}, s32[1,4096]{1,0:T(1,128)}, u32[]{:S(2)}) copy-start(s32[1,4096]{1,0:T(1,128)} %param.4) | copy-start | bytes 49156
  55.5 9.0 %collective-permute-start.6 = (f32[88,128]{1,0:T(8,128)S(1)}, f32[88,128]{1,0:T(8,128)S(1)}, u32[]{:S(2)}, u32[]{:S(2)}) collective-permute-start(f32[88,128]{1,0:T(8,128)S(1)} %collective-permute-done.5.p1), channel_id=1, source_target_pairs={{1,2},{2,1},{3,4},{4,3},{5,6},{6,5},{7,8},{8,7},{9,10},{10,9},{11,... | collective-permute-start | bytes 135176 | tf_op jit(solution)/shard_map/ppermute | solution.py:308
  58.9 6.1 %collective-permute-start.7 = (f32[88,128]{1,0:T(8,128)S(1)}, f32[88,128]{1,0:T(8,128)S(1)}, u32[]{:S(2)}, u32[]{:S(2)}) collective-permute-start(f32[88,128]{1,0:T(8,128)S(1)} %collective-permute-done.4.p0), channel_id=1, source_target_pairs={{0,1},{1,0},{2,3},{3,2},{4,5},{5,4},{6,7},{7,6},{8,9},{9,8},{10,11... | collective-permute-start | bytes 135176 | tf_op jit(solution)/shard_map/ppermute | solution.py:308

commit v7 on v6

--- a/solution.py
+++ b/solution.py
@@ -335,7 +335,7 @@
     layers = lax.axis_size("node") // CORES
     in_layer = [[z * layer + i for i in range(layer)] for z in range(layers)]
     across_layers = [[z * layer + i for z in range(layers)] for i in range(layer)]
-    lines = jax.ShapeDtypeStruct((layer, 4, LANES), f32)
+    lines = jax.ShapeDtypeStruct((layer, 1, 3 * LANES), f32)
     scratch = pltpu.VMEM((19, ROWS, LANES), f32)
     smem = [pl.BlockSpec(memory_space=pltpu.SMEM)]
     devices = lax.axis_size("node") * lax.axis_size("local")
@@ -364,7 +364,7 @@
     sums = spread_out(sums, in_layer)
     other, mate = exchange(pack)
     sums, mate = lax.optimization_barrier((sums, mate))
-    plane = jnp.sum(sums[:, 0, :], axis=0)[None, None]
+    plane = jnp.sum(sums[:, 0, :LANES], axis=0)[None, None]
     sums = spread_out(jnp.broadcast_to(plane, (layers, 2, LANES)), across_layers)
     other, mate, past_mate, past_other = pass_on(other, mate)
     tile = pl.pallas_call(

time: 67.9 us -> 67.9 us (level)
  no operation moved by 1% of the time
where the time goes in v7:
time: 67.9 us; the launch traced here: 67.4 us
  starting transfers between devices  52.2 us (77%)
  waiting for transfers between devices  7.35 us (11%)
  Pallas kernels  4.19 us (6%)
  local copies, waits for them, and re-layouts  2.29 us (3%)
  between operations  0.81 us (1%)
    ppermute x8, starting transfers between devices, swap(): return lax.ppermute(pack, ('node', 'local'), pairs)  31.1 us
    all_to_all x2, starting transfers between devices, spread_out(): lax.all_to_all(lines, ('node', 'local'), 0, 0, tiled=True, axis_index_gro...  21 us
    ppermute x8, waiting for transfers between devices, swap(): return lax.ppermute(pack, ('node', 'local'), pairs)  7.11 us
    pallas_call x1, Pallas kernels, shards(): pl.pallas_call(middle_kernel, out_shape=(cube, packed, lines), in_specs=v...  1.76 us
    unnamed x8, local copies, waits for them, and re-layouts  1.69 us
    pallas_call x1, Pallas kernels, shards(): pl.pallas_call(last_kernel, out_shape=cube, in_specs=vmem(2) + smem + vme...  1.56 us
  transfers between devices with their start and end apart: 10, of which 3 were waited for; matrix products, arithmetic and copies ran while one was open for 1% of the time, Pallas kernels for 3%

profile of v7, /device:TPU:1, one launch (start us, length us, event | category | flops | bytes accessed | tf_op | source)
XLA Modules:
  0.0 67.4 jit_solution(9427259980877437042)
XLA Ops:
  0.6 1.0 %copy-done = f32[1,19,4096]{2,0,1:T(1,128)S(1)} copy-done((f32[1,19,4096]{2,0,1:T(1,128)S(1)}, f32[1,19,4096]{2,0,1:T(1,128)}, u32[]{:S(2)}) %copy-start) | copy-done | bytes 311320
  1.6 0.7 %copy-done.1 = s32[1,4096]{1,0:T(1,128)S(1)} copy-done((s32[1,4096]{1,0:T(1,128)S(1)}, s32[1,4096]{1,0:T(1,128)}, u32[]{:S(2)}) %copy-start.1) | copy-done | bytes 16408
  2.3 0.3 collide_first.1
  2.6 4.2 %collective-permute-start.1 = (f32[88,128]{1,0:T(8,128)S(1)}, f32[88,128]{1,0:T(8,128)S(1)}, u32[]{:S(2)}, u32[]{:S(2)}) collective-permute-start(f32[88,128]{1,0:T(8,128)S(1)} %get-tuple-element.10), channel_id=1, source_target_pairs={{0,1},{1,0},{2,3},{3,2},{4,5},{5,4},{6,7},{7,6},{8,9},{9,8},{10,11... | collective-permute-start | bytes 135176 | tf_op jit(solution)/shard_map/ppermute | solution.py:308
  6.8 6.8 %collective-permute-start = (f32[88,128]{1,0:T(8,128)S(1)}, f32[88,128]{1,0:T(8,128)S(1)}, u32[]{:S(2)}, u32[]{:S(2)}) collective-permute-start(f32[88,128]{1,0:T(8,128)S(1)} %get-tuple-element.10), channel_id=1, source_target_pairs={{1,2},{2,1},{3,4},{4,3},{5,6},{6,5},{7,8},{8,7},{9,10},{10,9},{11,... | collective-permute-start | bytes 135176 | tf_op jit(solution)/shard_map/ppermute | solution.py:308
  13.6 0.0 collective-permute-done.1.p1
  13.6 3.3 %collective-permute-start.3 = (f32[88,128]{1,0:T(8,128)S(1)}, f32[88,128]{1,0:T(8,128)S(1)}, u32[]{:S(2)}, u32[]{:S(2)}) collective-permute-start(f32[88,128]{1,0:T(8,128)S(1)} %collective-permute-done.1.p1), channel_id=1, source_target_pairs={{1,2},{2,1},{3,4},{4,3},{5,6},{6,5},{7,8},{8,7},{9,10},{10,9},{11,... | collective-permute-start | bytes 135176 | tf_op jit(solution)/shard_map/ppermute | solution.py:308
  16.9 1.9 %collective-permute-start.2 = (f32[88,128]{1,0:T(8,128)S(1)}, f32[88,128]{1,0:T(8,128)S(1)}, u32[]{:S(2)}, u32[]{:S(2)}) collective-permute-start(f32[88,128]{1,0:T(8,128)S(1)} %collective-permute-done.p0), channel_id=1, source_target_pairs={{0,1},{1,0},{2,3},{3,2},{4,5},{5,4},{6,7},{7,6},{8,9},{9,8},{10,11... | collective-permute-start | bytes 135176 | tf_op jit(solution)/shard_map/ppermute | solution.py:308
  18.8 3.5 %collective-permute-done.3.p3 = f32[88,128]{1,0:T(8,128)S(1)} collective-permute-done((f32[88,128]{1,0:T(8,128)S(1)}, f32[88,128]{1,0:T(8,128)S(1)}, u32[]{:S(2)}, u32[]{:S(2)}) %collective-permute-start.3) | collective-permute-done | bytes 45088 | tf_op jit(solution)/shard_map/ppermute | solution.py:308
  22.3 1.8 %stream_collide.1 = (f32[19,32,128]{2,1,0:T(8,128)S(1)}, f32[88,128]{1,0:T(8,128)S(1)}, f32[32,1,384]{2,1,0:T(1,128)}) custom-call(f32[19,32,128]{2,1,0:T(8,128)S(1)} %get-tuple-element.9.own_ref, s32[32,128]{1,0:T(8,128)S(1)} %bitcast.5, s32[1,6]{1,0:T(1,128)S(1)} %copy-done.3, f32[88,128]{1,0:T(8,128)S(1)} %collective-permute-done.p0, ...), custom_call_target="tpu_custom_call" | custom-call | tf_op jit(solution)/shard_map/stream_collide/pallas_call | solution.py:355
  24.1 6.1 %all-to-all-start = ((f32[32,1,384]{2,1,0:T(1,128)}), f32[32,1,384]{2,1,0:T(1,128)S(1)}, u32[]{:S(2)}, u32[]{:S(2)}) async-start(f32[32,1,384]{2,1,0:T(1,128)} %get-tuple-element.13), calls=%async_computation | async-start | bytes 98304 | tf_op jit(solution)/shard_map/all_to_all | solution.py:327
  30.2 3.3 %collective-permute-start.5 = (f32[88,128]{1,0:T(8,128)S(1)}, f32[88,128]{1,0:T(8,128)S(1)}, u32[]{:S(2)}, u32[]{:S(2)}) collective-permute-start(f32[88,128]{1,0:T(8,128)S(1)} %get-tuple-element.12), channel_id=1, source_target_pairs={{0,1},{1,0},{2,3},{3,2},{4,5},{5,4},{6,7},{7,6},{8,9},{9,8},{10,11... | collective-permute-start | bytes 135176 | tf_op jit(solution)/shard_map/ppermute | solution.py:308
  33.5 6.3 %collective-permute-start.4 = (f32[88,128]{1,0:T(8,128)S(1)}, f32[88,128]{1,0:T(8,128)S(1)}, u32[]{:S(2)}, u32[]{:S(2)}) collective-permute-start(f32[88,128]{1,0:T(8,128)S(1)} %get-tuple-element.12), channel_id=1, source_target_pairs={{1,2},{2,1},{3,4},{4,3},{5,6},{6,5},{7,8},{8,7},{9,10},{10,9},{11,... | collective-permute-start | bytes 135176 | tf_op jit(solution)/shard_map/ppermute | solution.py:308
  39.8 0.0 collective-permute-done.5.p1
  39.9 0.6 broadcast_in_dim.2
  40.5 14.9 %all-to-all-start.1 = ((f32[16,2,128]{2,1,0:T(2,128)}), f32[16,2,128]{2,1,0:T(2,128)S(1)}, u32[]{:S(2)}, u32[]{:S(2)}) async-start(f32[16,2,128]{2,1,0:T(2,128)} %broadcast_in_dim.2), calls=%async_computation.1 | async-start | bytes 32768 | tf_op jit(solution)/shard_map/all_to_all | solution.py:327
  55.4 0.0 copy-start.2
  55.5 3.4 %collective-permute-start.6 = (f32[88,128]{1,0:T(8,128)S(1)}, f32[88,128]{1,0:T(8,128)S(1)}, u32[]{:S(2)}, u32[]{:S(2)}) collective-permute-start(f32[88,128]{1,0:T(8,128)S(1)} %collective-permute-done.5.p1), channel_id=1, source_target_pairs={{1,2},{2,1},{3,4},{4,3},{5,6},{6,5},{7,8},{8,7},{9,10},{10,9},{11,... | collective-permute-start | bytes 135176 | tf_op jit(solution)/shard_map/ppermute | solution.py:308
  58.9 1.9 %collective-permute-start.7 = (f32[88,128]{1,0:T(8,128)S(1)}, f32[88,128]{1,0:T(8,128)S(1)}, u32[]{:S(2)}, u32[]{:S(2)}) collective-permute-start(f32[88,128]{1,0:T(8,128)S(1)} %collective-permute-done.4.p0), channel_id=1, source_target_pairs={{0,1},{1,0},{2,3},{3,2},{4,5},{5,4},{6,7},{7,6},{8,9},{9,8},{10,11... | collective-permute-start | bytes 135176 | tf_op jit(solution)/shard_map/ppermute | solution.py:308
  60.8 3.6 %collective-permute-done.6.p3 = f32[88,128]{1,0:T(8,128)S(1)} collective-permute-done((f32[88,128]{1,0:T(8,128)S(1)}, f32[88,128]{1,0:T(8,128)S(1)}, u32[]{:S(2)}, u32[]{:S(2)}) %collective-permute-start.6) | collective-permute-done | bytes 45088 | tf_op jit(solution)/shard_map/ppermute | solution.py:308
  64.4 0.6 pick_tiles.1.base_ref
  65.0 1.6 %stream_last.1 = f32[19,32,128]{2,1,0:T(8,128)} custom-call(f32[19,32,128]{2,1,0:T(8,128)S(1)} %get-tuple-element.11.own_ref, s32[32,128]{1,0:T(8,128)S(1)} %bitcast.6, s32[1,6]{1,0:T(1,128)S(1)} %copy-done.3, f32[88,128]{1,0:T(8,128)S(1)} %pick_tiles.1.base_ref, f32[88,128]{1,0:T(8,128)S(1)} %collective-permute-done.7.p2), custom_call_target="tpu_custom_call" | custom-call | flops 4000000 | bytes 1000000 | tf_op jit(solution)/shard_map/stream_last/pallas_call | solution.py:379
  66.6 0.2 all-to-all-done.1
  66.9 0.5 broadcast_multiply_fusion
  (12 shorter events, 0.1 us)
Async XLA Ops:
  0.6 1.0 %copy-start = (f32[1,19,4096]{2,0,1:T(1,128)S(1)}, f32[1,19,4096]{2,0,1:T(1,128)}, u32[]{:S(2)}) copy-start(f32[1,19,4096]{2,0,1:T(1,128)} %param.3) | copy-start | bytes 933892
  1.6 0.7 %copy-start.1 = (s32[1,4096]{1,0:T(1,128)S(1)}, s32[1,4096]{1,0:T(1,128)}, u32[]{:S(2)}) copy-start(s32[1,4096]{1,0:T(1,128)} %param.4) | copy-start | bytes 49156
  2.6 19.7 %copy-start.3 = (s32[1,6]{1,0:T(1,128)S(1)}, s32[1,6]{1,0:T(1,128)}, u32[]{:S(2)}) copy-start(s32[1,6]{1,0:T(1,128)} %nb_ref.5) | copy-start | bytes 76
  2.6 11.0 %collective-permute-start.1 = (f32[88,128]{1,0:T(8,128)S(1)}, f32[88,128]{1,0:T(8,128)S(1)}, u32[]{:S(2)}, u32[]{:S(2)}) collective-permute-start(f32[88,128]{1,0:T(8,128)S(1)} %get-tuple-element.10), channel_id=1, source_target_pairs={{0,1},{1,0},{2,3},{3,2},{4,5},{5,4},{6,7},{7,6},{8,9},{9,8},{10,11... | collective-permute-start | bytes 135176 | tf_op jit(solution)/shard_map/ppermute | solution.py:308
  6.8 10.1 %collective-permute-start = (f32[88,128]{1,0:T(8,128)S(1)}, f32[88,128]{1,0:T(8,128)S(1)}, u32[]{:S(2)}, u32[]{:S(2)}) collective-permute-start(f32[88,128]{1,0:T(8,128)S(1)} %get-tuple-element.10), channel_id=1, source_target_pairs={{1,2},{2,1},{3,4},{4,3},{5,6},{6,5},{7,8},{8,7},{9,10},{10,9},{11,... | collective-permute-start | bytes 135176 | tf_op jit(solution)/shard_map/ppermute | solution.py:308
  13.6 8.7 %collective-permute-start.3 = (f32[88,128]{1,0:T(8,128)S(1)}, f32[88,128]{1,0:T(8,128)S(1)}, u32[]{:S(2)}, u32[]{:S(2)}) collective-permute-start(f32[88,128]{1,0:T(8,128)S(1)} %collective-permute-done.1.p1), channel_id=1, source_target_pairs={{1,2},{2,1},{3,4},{4,3},{5,6},{6,5},{7,8},{8,7},{9,10},{10,9},{11,... | collective-permute-start | bytes 135176 | tf_op jit(solution)/shard_map/ppermute | solution.py:308
  16.9 5.4 %collective-permute-start.2 = (f32[88,128]{1,0:T(8,128)S(1)}, f32[88,128]{1,0:T(8,128)S(1)}, u32[]{:S(2)}, u32[]{:S(2)}) collective-permute-start(f32[88,128]{1,0:T(8,128)S(1)} %collective-permute-done.p0), channel_id=1, source_target_pairs={{0,1},{1,0},{2,3},{3,2},{4,5},{5,4},{6,7},{7,6},{8,9},{9,8},{10,11... | collective-permute-start | bytes 135176 | tf_op jit(solution)/shard_map/ppermute | solution.py:308
  24.1 15.7 %all-to-all-start = ((f32[32,1,384]{2,1,0:T(1,128)}), f32[32,1,384]{2,1,0:T(1,128)S(1)}, u32[]{:S(2)}, u32[]{:S(2)}) async-start(f32[32,1,384]{2,1,0:T(1,128)} %get-tuple-element.13), calls=%async_computation | async-start | bytes 98304 | tf_op jit(solution)/shard_map/all_to_all | solution.py:327
  30.2 9.6 %collective-permute-start.5 = (f32[88,128]{1,0:T(8,128)S(1)}, f32[88,128]{1,0:T(8,128)S(1)}, u32[]{:S(2)}, u32[]{:S(2)}) collective-permute-start(f32[88,128]{1,0:T(8,128)S(1)} %get-tuple-element.12), channel_id=1, source_target_pairs={{0,1},{1,0},{2,3},{3,2},{4,5},{5,4},{6,7},{7,6},{8,9},{9,8},{10,11... | collective-permute-start | bytes 135176 | tf_op jit(solution)/shard_map/ppermute | solution.py:308
  33.5 25.4 %collective-permute-start.4 = (f32[88,128]{1,0:T(8,128)S(1)}, f32[88,128]{1,0:T(8,128)S(1)}, u32[]{:S(2)}, u32[]{:S(2)}) collective-permute-start(f32[88,128]{1,0:T(8,128)S(1)} %get-tuple-element.12), channel_id=1, source_target_pairs={{1,2},{2,1},{3,4},{4,3},{5,6},{6,5},{7,8},{8,7},{9,10},{10,9},{11,... | collective-permute-start | bytes 135176 | tf_op jit(solution)/shard_map/ppermute | solution.py:308
  40.5 26.3 %all-to-all-start.1 = ((f32[16,2,128]{2,1,0:T(2,128)}), f32[16,2,128]{2,1,0:T(2,128)S(1)}, u32[]{:S(2)}, u32[]{:S(2)}) async-start(f32[16,2,128]{2,1,0:T(2,128)} %broadcast_in_dim.2), calls=%async_computation.1 | async-start | bytes 32768 | tf_op jit(solution)/shard_map/all_to_all | solution.py:327
  55.4 9.6 %copy-start.2 = (s32[1,4096]{1,0:T(1,128)S(1)}, s32[1,4096]{1,0:T(1,128)}, u32[]{:S(2)}) copy-start(s32[1,4096]{1,0:T(1,128)} %param.4) | copy-start | bytes 49156
  55.5 9.0 %collective-permute-start.6 = (f32[88,128]{1,0:T(8,128)S(1)}, f32[88,128]{1,0:T(8,128)S(1)}, u32[]{:S(2)}, u32[]{:S(2)}) collective-permute-start(f32[88,128]{1,0:T(8,128)S(1)} %collective-permute-done.5.p1), channel_id=1, source_target_pairs={{1,2},{2,1},{3,4},{4,3},{5,6},{6,5},{7,8},{8,7},{9,10},{10,9},{11,... | collective-permute-start | bytes 135176 | tf_op jit(solution)/shard_map/ppermute | solution.py:308
  58.9 6.1 %collective-permute-start.7 = (f32[88,128]{1,0:T(8,128)S(1)}, f32[88,128]{1,0:T(8,128)S(1)}, u32[]{:S(2)}, u32[]{:S(2)}) collective-permute-start(f32[88,128]{1,0:T(8,128)S(1)} %collective-permute-done.4.p0), channel_id=1, source_target_pairs={{0,1},{1,0},{2,3},{3,2},{4,5},{5,4},{6,7},{7,6},{8,9},{9,8},{10,11... | collective-permute-start | bytes 135176 | tf_op jit(solution)/shard_map/ppermute | solution.py:308
